TPU v7x, 512 devices: a whole 4x8x8 slice. The times are simulated.
512 devices in a mesh: ctx: 64 (over y, z_lo, x), head: 8 (over z_hi, core).
Axes of the slice: x: 4, y: 8, z: 8 (z_hi: 4, z_lo: 2; z = z_hi * 2 + z_lo), core: 2. Of those that a mesh axis runs over, the one named last changes fastest.
Arguments:
- queries: bfloat16 [8192, 8192], P(('ctx', 'head')), may hold values from -8 to 8
- keys: bfloat16 [8192, 1024], P(('ctx', 'head')), may hold values from -8 to 8
- values: bfloat16 [8192, 1024], P(('ctx', 'head')), may hold values from -6 to 6
- output_gradient: bfloat16 [8192, 8192], P('ctx', 'head'), may hold values from -6 to 6
- segment_ids: int32 [8192], replicated, may hold values from 0 to 23, never falling along the last dimension, each value on 1 to 512 neighbouring positions
- block_order: int32 [128], replicated, may hold values from 0 to 127, each once
Outputs:
- attended: bfloat16 [8192, 8192], P('ctx', 'head')
- grad_queries: bfloat16 [8192, 8192], P(('ctx', 'head'))
- key_gradient: bfloat16 [8192, 1024], P(('ctx', 'head'))
- value_gradient: bfloat16 [8192, 1024], P(('ctx', 'head'))
Inputs may be any that keep to these rules, and one draw needn't show every extreme that they name: `segment_ids`: labels never fall along the sequence; each rollout holds 1 to 512 positions and one holds exactly 512. `block_order`: each of the 128 sequence blocks is held once.
All inputs are finite; a program needn't handle non-finite values.
Results may differ from a plain program's by a relative error of at most 0.035.
Values may be sent and summed in bfloat16 or wider, within the bound.
A program may use at most 64 MiB of HBM per device.

v0:
```python
import jax
import jax.numpy as jnp
from jax import lax
from jax.sharding import PartitionSpec as P

HEAD_SPAN = 128
DOC_MOST = 512
HALF = 64


masked_score = -1e30


def as_sent(x):
    return jax.tree.map(lambda a: a.astype(jnp.bfloat16) if a.dtype == jnp.float32 else a, x)


def from_behind(x, axis, by):
    length = lax.axis_size(axis)
    return lax.ppermute(x, axis, [(i, (i + by) % length) for i in range(length)])


def block_places(segment_ids, block_order, owner_upper, owner_lower):
    offsets = jnp.arange(HALF, dtype=jnp.int32)
    start_upper = block_order[2 * owner_upper] * HALF
    start_lower = block_order[2 * owner_lower + 1] * HALF
    places = jnp.concatenate([start_upper + offsets, start_lower + offsets])
    labels = jnp.concatenate(
        [
            lax.dynamic_slice_in_dim(segment_ids, start_upper, HALF),
            lax.dynamic_slice_in_dim(segment_ids, start_lower, HALF),
        ]
    )
    return (places, labels)


def pass_keys(moving):
    return jax.tree.map(
        lambda part, own: part.astype(own.dtype), from_behind(as_sent(moving), "ctx", 1), moving
    )


def pass_grads(accum):
    return from_behind(as_sent(accum), "ctx", 1).astype(accum.dtype)


def shards(queries, keys, values, output_gradient, segment_ids, block_order):
    query_local, key_local, value_local = (
        lax.all_to_all(queries, "head", split_axis=1, concat_axis=0, tiled=True),
        lax.all_to_all(keys, "head", split_axis=1, concat_axis=0, tiled=True),
        lax.all_to_all(values, "head", split_axis=1, concat_axis=0, tiled=True),
    )
    query_rows = query_local.shape[0]
    head_dim = HEAD_SPAN
    kv_heads = key_local.shape[1] // head_dim
    group_count = query_local.shape[1] // head_dim // kv_heads
    group_width = group_count * head_dim
    score_scale = head_dim ** (-0.5)
    cycle_size = lax.axis_size("ctx")
    cycle_index = lax.axis_index("ctx")
    store_size = min(cycle_size, 2 * (DOC_MOST // HALF + 1))
    direction_sign = 1
    query_parts = [query_local.reshape(query_rows * group_count, head_dim)]
    grad_parts = [output_gradient.reshape(query_rows * group_count, head_dim)]
    query_places, query_labels = block_places(segment_ids, block_order, cycle_index, cycle_index)

    def allowed_at(step):
        owner_upper = (cycle_index - step) % cycle_size
        owner_lower = (cycle_index - direction_sign * step) % cycle_size
        key_places, key_labels = block_places(segment_ids, block_order, owner_upper, owner_lower)
        return (query_labels[:, None] == key_labels[None, :]) & (
            key_places[None, :] <= query_places[:, None]
        )

    def tile_scores(index, key_tile, allowed):
        key_part = key_tile[:, index * head_dim : (index + 1) * head_dim]
        scores = jnp.einsum(
            "rd,kd->rk", query_parts[index], key_part, preferred_element_type=jnp.float32
        )
        scores = scores.reshape(query_rows, group_count, -1) * score_scale
        return jnp.where(allowed[:, None, :], scores, masked_score)

    def soft_tile(soft, key_tile, value_tile, allowed):
        maxima, totals, sums = soft
        new_maxima, new_totals, new_sums = ([], [], [])
        scores = tile_scores(0, key_tile, allowed)
        top = jnp.maximum(maxima[0], jnp.max(scores, axis=-1))
        raised = jnp.where(allowed[:, None, :], jnp.exp(scores - top[..., None]), 0.0)
        decay = jnp.exp(maxima[0] - top)
        new_totals.append(totals[0] * decay + jnp.sum(raised, axis=-1))
        weights = raised.astype(jnp.bfloat16).reshape(query_rows * group_count, -1)
        value_part = value_tile[:, 0:head_dim]
        product = jnp.dot(weights, value_part, preferred_element_type=jnp.float32).reshape(
            query_rows, group_count, head_dim
        )
        new_sums.append(sums[0] * decay[..., None] + product)
        new_maxima.append(top)
        return (tuple(new_maxima), tuple(new_totals), tuple(new_sums))

    kv_width = key_local.shape[1]
    soft_start = (
        tuple(
            (
                jnp.full((query_rows, group_count), masked_score, jnp.float32)
                for index in range(kv_heads)
            )
        ),
        tuple((jnp.zeros((query_rows, group_count), jnp.float32) for index in range(kv_heads))),
        tuple(
            (
                jnp.zeros((query_rows, group_count, head_dim), jnp.float32)
                for index in range(kv_heads)
            )
        ),
    )
    moving = jnp.stack([key_local, value_local])
    store_start = (
        jnp.zeros((store_size, query_rows, kv_width), jnp.bfloat16),
        jnp.zeros((store_size, query_rows, kv_width), jnp.bfloat16),
        jnp.full((store_size,), -1, jnp.int32),
        jnp.zeros((), jnp.int32),
    )

    def cycle_visit(step, soft, store, tile):
        allowed = allowed_at(step)

        def take(inner):
            inner_soft, inner_store = inner
            store_keys, store_values, store_steps, filled = inner_store
            new_soft = soft_tile(inner_soft, tile[0], tile[1], allowed)
            store_keys = lax.dynamic_update_index_in_dim(store_keys, tile[0], filled, 0)
            store_values = lax.dynamic_update_index_in_dim(store_values, tile[1], filled, 0)
            store_steps = store_steps.at[filled].set(step)
            return (new_soft, (store_keys, store_values, store_steps, filled + 1))

        return lax.cond(jnp.any(allowed), take, lambda inner: inner, (soft, store))

    soft, store = cycle_visit(0, soft_start, store_start, moving)

    def cycle_step(step, carry):
        moving_now, soft_now, store_now = carry
        moving_now = pass_keys(moving_now)
        soft_now, store_now = cycle_visit(step, soft_now, store_now, moving_now)
        return (moving_now, soft_now, store_now)

    moving, soft, store = lax.fori_loop(1, cycle_size, cycle_step, (moving, soft, store))
    store_keys, store_values, store_steps, filled = store

    def fetch_tile(step):
        slot_hits = store_steps == step
        slot = jnp.sum(jnp.where(slot_hits, jnp.arange(store_size, dtype=jnp.int32), 0))
        key_tile = lax.dynamic_index_in_dim(store_keys, slot, 0, keepdims=False)
        value_tile = lax.dynamic_index_in_dim(store_values, slot, 0, keepdims=False)
        return (jnp.any(slot_hits), key_tile, value_tile)

    maxima, totals, sums = soft
    attended = jnp.concatenate(
        [(sums[0] / totals[0][..., None]).reshape(query_rows, group_width)], axis=1
    ).astype(jnp.bfloat16)
    dsum_all = jnp.sum(
        (output_gradient.astype(jnp.float32) * attended.astype(jnp.float32)).reshape(
            query_rows, kv_heads, group_count, head_dim
        ),
        axis=-1,
    )

    def backward_tile(carried, key_tile, value_tile, allowed):
        query_grads, accum = carried
        key_grads, value_grads, new_query_grads = ([], [], [])
        scores = tile_scores(0, key_tile, allowed)
        probs = jnp.where(
            allowed[:, None, :], jnp.exp(scores - maxima[0][..., None]) / totals[0][..., None], 0.0
        )
        probs_b = probs.astype(jnp.bfloat16).reshape(query_rows * group_count, -1)
        value_grads.append(
            jnp.einsum("rk,rd->kd", probs_b, grad_parts[0], preferred_element_type=jnp.float32)
        )
        value_part = value_tile[:, 0:head_dim]
        dprobs = jnp.einsum(
            "rd,kd->rk", grad_parts[0], value_part, preferred_element_type=jnp.float32
        ).reshape(query_rows, group_count, -1)
        dscores = (
            (probs * (dprobs - dsum_all[:, 0][..., None]))
            .astype(jnp.bfloat16)
            .reshape(query_rows * group_count, -1)
        )
        key_part = key_tile[:, 0:head_dim]
        new_query_grads.append(
            query_grads[0]
            + score_scale * jnp.dot(dscores, key_part, preferred_element_type=jnp.float32)
        )
        key_grads.append(
            score_scale
            * jnp.einsum("rk,rd->kd", dscores, query_parts[0], preferred_element_type=jnp.float32)
        )
        update = jnp.stack(
            [jnp.concatenate(key_grads, axis=1), jnp.concatenate(value_grads, axis=1)]
        )
        return (tuple(new_query_grads), accum + update)

    def backward_step(step, carry):
        allowed = allowed_at(step)
        present, key_tile, value_tile = fetch_tile(step)
        query_grads, accum = lax.cond(
            present,
            lambda inner: backward_tile(inner, key_tile, value_tile, allowed),
            lambda inner: inner,
            carry,
        )
        return (query_grads, pass_grads(accum))

    start_grads = (
        tuple(
            (
                jnp.zeros((query_rows * group_count, head_dim), jnp.float32)
                for index in range(kv_heads)
            )
        ),
        jnp.zeros((2, query_rows, kv_width), jnp.float32),
    )
    query_grads, accum = lax.fori_loop(0, cycle_size, backward_step, start_grads)
    grad_queries = query_grads[0].reshape(query_rows, group_width).astype(jnp.bfloat16)
    key_gradient = accum[0].astype(jnp.bfloat16)
    value_gradient = accum[1].astype(jnp.bfloat16)
    grad_queries, key_gradient, value_gradient = (
        lax.all_to_all(grad_queries, "head", split_axis=0, concat_axis=1, tiled=True),
        lax.all_to_all(key_gradient, "head", split_axis=0, concat_axis=1, tiled=True),
        lax.all_to_all(value_gradient, "head", split_axis=0, concat_axis=1, tiled=True),
    )
    return (attended, grad_queries, key_gradient, value_gradient)


def solution(mesh):
    in_specs = (
        P(("ctx", "head"), None),
        P(("ctx", "head"), None),
        P(("ctx", "head"), None),
        P("ctx", "head"),
        P(),
        P(),
    )
    out_specs = (
        P("ctx", "head"),
        P(("ctx", "head"), None),
        P(("ctx", "head"), None),
        P(("ctx", "head"), None),
    )
    return jax.shard_map(shards, mesh=mesh, in_specs=in_specs, out_specs=out_specs, check_vma=False)
```

profile of v0, /device:TPU:1, one launch (start us, length us, event | category | flops | bytes accessed | tf_op | source)
XLA Modules:
  0.0 1740.2 jit_solution(17574330154744580454)
XLA Ops:
  2.0 11.8 all-to-all-start
  41.3 8.5 all-to-all-done.2
  52.2 593.6 %while.49 = (s32[]{:T(128)}, bf16[2,128,128]{2,1,0:T(8,128)(2,1)S(1)}, f32[128,8]{0,1:T(8,128)S(1)}, f32[128,8]{0,1:T(8,128)S(1)}, f32[128,8,128]{2,0,1:T(8,128)...) while((s32[]{:T(128)}, ...), condition=%wide.region_11.12_spmd, body=%wide.region_5.11_spmd.sunk | while | flops 68618656 | bytes 3611148 | solution.py:146
  647.2 910.1 %while.50 = (s32[]{:T(128)}, f32[1024,128]{1,0:T(8,128)S(1)}, f32[2,128,128]{2,1,0:T(8,128)S(1)}, s32[18]{0:T(128)S(1)}, s32[]{:T(128)}, /*index=5*/s32[128]{0:T...) while((s32[]{:T(128)}, f32[1024,128]{1,0:T(8,128)S(1)}, ...), condition=%wide.region_18.19_spmd.clone, body=%wide.region_13.0_spmd.clone.sunk | while | flops 169443808 | bytes 6597184 | solution.py:221
  658.1 7.3 collective-permute-done.1
  676.2 7.3 collective-permute-done.1
  694.2 7.3 collective-permute-done.1
  712.3 7.6 collective-permute-done.1
  726.1 7.3 collective-permute-done.1
  753.1 7.3 collective-permute-done.1
  766.6 7.3 collective-permute-done.1
  780.0 7.3 collective-permute-done.1
  793.5 7.3 collective-permute-done.1
  807.0 7.3 collective-permute-done.1
  820.5 7.4 collective-permute-done.1
  834.2 7.7 collective-permute-done.1
  852.7 7.3 collective-permute-done.1
  866.2 7.3 collective-permute-done.1
  879.7 7.3 collective-permute-done.1
  897.8 7.3 collective-permute-done.1
  911.3 7.3 collective-permute-done.1
  924.8 7.3 collective-permute-done.1
  938.3 7.3 collective-permute-done.1
  956.4 8.0 collective-permute-done.1
  970.6 7.3 collective-permute-done.1
  984.1 7.3 collective-permute-done.1
  997.6 7.3 collective-permute-done.1
  1011.1 7.3 collective-permute-done.1
  1024.7 7.3 collective-permute-done.1
  1038.1 7.3 collective-permute-done.1
  1056.2 7.3 collective-permute-done.1
  1069.7 7.3 collective-permute-done.1
  1083.2 8.0 collective-permute-done.1
  1097.4 7.3 collective-permute-done.1
  1124.4 7.3 collective-permute-done.1
  1137.9 7.3 collective-permute-done.1
  1151.4 7.3 collective-permute-done.1
  1164.9 7.3 collective-permute-done.1
  1178.4 7.3 collective-permute-done.1
  1191.9 7.3 collective-permute-done.1
  1205.4 8.0 collective-permute-done.1
  1219.5 7.3 collective-permute-done.1
  1233.0 7.3 collective-permute-done.1
  1246.5 7.3 collective-permute-done.1
  1264.6 8.3 collective-permute-done.1
  1279.1 7.3 collective-permute-done.1
  1292.6 7.3 collective-permute-done.1
  1306.0 7.3 collective-permute-done.1
  1319.5 7.3 collective-permute-done.1
  1333.0 7.3 collective-permute-done.1
  1346.5 7.3 collective-permute-done.1
  1360.0 7.3 collective-permute-done.1
  1373.5 7.3 collective-permute-done.1
  1387.0 8.2 collective-permute-done.1
  1401.5 7.3 collective-permute-done.1
  1415.0 7.3 collective-permute-done.1
  1428.6 7.3 collective-permute-done.1
  1442.0 7.3 collective-permute-done.1
  1455.5 7.3 collective-permute-done.1
  1469.0 7.3 collective-permute-done.1
  1536.5 7.3 collective-permute-done.1
  1550.1 7.3 collective-permute-done.1
  1558.0 155.9 %all_to_all.102 = bf16[8,16,128]{2,1,0:T(8,128)(2,1)S(1)} all-to-all(bf16[8,16,128]{2,1,0:T(8,128)(2,1)S(1)} %bitcast.152), channel_id=1, replica_groups=mesh['ctx'=64,'head'=8] {'head'}, dimensions={0} | all-to-all | bytes 65536 | tf_op jit(solution)/shard_map/all_to_all | solution.py:228
  1731.1 8.4 all-to-all-done.3
  (1645 shorter events, 897.8 us)
Async XLA Ops:
  2.0 19.1 %all-to-all-start = ((bf16[16,8,128]{2,0,1:T(8,128)(2,1)}), bf16[16,8,128]{2,0,1:T(8,128)(2,1)S(1)}, u32[]{:S(2)}, u32[]{:S(2)}) async-start(bf16[16,8,128]{2,0,1:T(8,128)(2,1)} %copy_bitcast_fusion.5), calls=%async_computation | async-start | bytes 65536 | tf_op jit(solution)/shard_map/all_to_all | solution.py:50
  21.1 14.3 all-to-all-start.1
  35.5 14.3 all-to-all-start.2
  52.2 10.2 collective-permute-start
  63.5 9.2 collective-permute-start
  73.8 9.2 collective-permute-start
  84.1 9.2 collective-permute-start
  121.0 9.7 collective-permute-start
  177.9 9.2 collective-permute-start
  206.7 9.2 collective-permute-start
  215.9 9.7 collective-permute-start
  245.1 9.2 collective-permute-start
  291.3 9.5 collective-permute-start
  311.1 9.2 collective-permute-start
  375.7 9.6 collective-permute-start
  451.0 9.2 collective-permute-start
  469.4 9.6 collective-permute-start
  543.6 9.5 collective-permute-start
  627.0 9.6 collective-permute-start
  656.1 9.2 collective-permute-start.1
  674.2 9.2 collective-permute-start.1
  692.3 9.2 collective-permute-start.1
  710.4 9.5 collective-permute-start.1
  724.1 9.2 collective-permute-start.1
  737.6 9.2 collective-permute-start.1
  751.1 9.2 collective-permute-start.1
  764.6 9.2 collective-permute-start.1
  778.1 9.2 collective-permute-start.1
  791.6 9.2 collective-permute-start.1
  805.1 9.2 collective-permute-start.1
  818.6 9.4 collective-permute-start.1
  832.2 9.6 collective-permute-start.1
  850.8 9.2 collective-permute-start.1
  864.3 9.2 collective-permute-start.1
  877.8 9.2 collective-permute-start.1
  895.9 9.2 collective-permute-start.1
  909.4 9.2 collective-permute-start.1
  922.9 9.2 collective-permute-start.1
  936.4 9.2 collective-permute-start.1
  954.5 10.0 collective-permute-start.1
  968.7 9.2 collective-permute-start.1
  982.2 9.2 collective-permute-start.1
  995.7 9.2 collective-permute-start.1
  1054.3 9.2 collective-permute-start.1
  1067.8 9.2 collective-permute-start.1
  1081.3 10.0 collective-permute-start.1
  1136.0 9.2 collective-permute-start.1
  1149.5 9.2 collective-permute-start.1
  1163.0 9.2 collective-permute-start.1
  1203.5 9.9 collective-permute-start.1
  1262.7 10.2 collective-permute-start.1
  1331.1 9.2 collective-permute-start.1
  1344.6 9.2 collective-permute-start.1
  1358.1 9.2 collective-permute-start.1
  1371.6 9.2 collective-permute-start.1
  1385.1 10.2 collective-permute-start.1
  1399.5 9.2 collective-permute-start.1
  1413.1 9.2 collective-permute-start.1
  1426.6 9.2 collective-permute-start.1
  1440.1 9.2 collective-permute-start.1
  1534.6 9.2 collective-permute-start.1
  1548.1 9.2 collective-permute-start.1
  1713.9 11.2 all-to-all-start.4
  1725.1 14.4 all-to-all-start.3
  (73 other events, 636.5 us)
where the time goes:
time: 1760 us; the launch traced here: 1740 us
  waiting for transfers between devices  694 us (39%)
  loops' own time  279 us (16%)
  starting transfers between devices  277 us (16%)
  local copies, waits for them, and re-layouts  192 us (11%)
  blocking collectives  156 us (9%)
  other arithmetic  121 us (7%)
    ppermute x127, waiting for transfers between devices, from_behind(): lax.ppermute(x, axis, [(i, (i + by) % length) for i in range(length)])  664 us
    ppermute x127, starting transfers between devices, from_behind(): lax.ppermute(x, axis, [(i, (i + by) % length) for i in range(length)])  246 us
    all_to_all x1, blocking collectives, shards(): lax.all_to_all(value_gradient, 'head', split_axis=0, concat_axis=1, tiled...  156 us
    another operation x1, loops' own time, shards(): lax.fori_loop(0, cycle_size, backward_step, start_grads)  132 us
    another operation x1, loops' own time, shards(): lax.fori_loop(1, cycle_size, cycle_step, (moving, soft, store))  127 us
    dynamic_slice x128, local copies, waits for them, and re-layouts, block_places(): lax.dynamic_slice_in_dim(segment_ids, start_upper, HALF)  101 us
    dynamic_slice x128, local copies, waits for them, and re-layouts, block_places(): start_upper = block_order[2 * owner_upper] * HALF  75.8 us
    reduce_or x64, other arithmetic, cycle_visit(): return lax.cond(jnp.any(allowed), take, lambda inner: inner, (soft, store))  47.2 us
  transfers between devices with their start and end apart: 132, of which 132 were waited for; matrix products, arithmetic and copies ran while one was open for 9% of the time, Pallas kernels for 0%

commit v1 on v0

v1 whole, which is shorter than its diff:
```python
import functools

import jax
import jax.numpy as jnp
import numpy as np
from jax import lax
from jax.experimental import pallas as pl
from jax.experimental.pallas import tpu as pltpu
from jax.sharding import PartitionSpec as P

SPAN = 128
BLOCK = 64
GROUP = 8
BACK = 8
SEEN = BACK + 1
WINDOW = SEEN * BLOCK
LINE = 4
PAIR = 2
CLASSES = 16
PIECES = 8
PART = SEEN * 8
LANES = 256
NEVER = -1e30

MESH = pl.DeviceIdType.MESH
NT = (((1,), (1,)), ((), ()))
TN = (((0,), (0,)), ((), ()))


def rank_of(c):
    return (lax.rem(c // LINE, PAIR)) * PIECES + lax.rem(c // (LINE * PAIR), 2) * LINE + lax.rem(c, LINE)


def member(c, e):
    x = lax.rem(lax.rem(c, LINE) + lax.rem(e, LINE), LINE)
    z = lax.rem(lax.rem(c // LINE, PAIR) + lax.rem(e // LINE, PAIR), PAIR)
    y = lax.rem(lax.rem(c // (LINE * PAIR), 2) + e // (LINE * PAIR), 2)
    return (c // CLASSES) * CLASSES + (y * PAIR + z) * LINE + x


def await_bytes(ref, sem):
    pltpu.make_async_copy(ref, ref, sem).wait()


def kernel(
    nc, nh,
    order, place, q_ref, k_ref, v_ref, do_ref, seg_ref,
    att_out, dq_out, dk_out, dv_out,
    q_loc, kv_loc, spread, r1, stored, seq, s2, r2, keys, vals, dot_t, bias,
    probs, dscores, dq_loc, s3, r3, r3f, acc, s4, r4, dkv_loc,
    send_sem, recv_sem,
):
    c = lax.axis_index("ctx")
    h = lax.axis_index("head")
    rows = q_ref.shape[0]
    wide = GROUP * SPAN
    blocks = 2 * nc
    f32, bf16 = jnp.float32, jnp.bfloat16

    def remote(src, dst, which, where):
        return pltpu.make_async_remote_copy(
            src_ref=src, dst_ref=dst, send_sem=send_sem.at[which], recv_sem=recv_sem.at[which],
            device_id=where, device_id_type=MESH,
        )

    barrier = pltpu.get_barrier_semaphore()

    def greet_ctx(d, _):
        pl.semaphore_signal(barrier, inc=1, device_id={"ctx": lax.rem(c + d, nc)}, device_id_type=MESH)
        return 0

    def greet_head(d, _):
        pl.semaphore_signal(barrier, inc=1, device_id={"head": lax.rem(h + d, nh)}, device_id_type=MESH)
        return 0

    lax.fori_loop(1, nh, greet_head, 0)
    lax.fori_loop(1, nc, greet_ctx, 0)
    pl.semaphore_wait(barrier, nc - 1 + nh - 1)

    def own_rows(g):
        return pl.ds(pl.multiple_of(g * rows, rows), rows)

    def head_columns(g, width):
        return pl.ds(pl.multiple_of(g * width, width), width)

    def send_kv(d, _):
        g = lax.rem(h + d, nh)
        remote(k_ref.at[:, head_columns(g, SPAN)], kv_loc.at[0, own_rows(h), :], 0, {"head": g}).start()
        remote(v_ref.at[:, head_columns(g, SPAN)], kv_loc.at[1, own_rows(h), :], 0, {"head": g}).start()
        return 0

    lax.fori_loop(1, nh, send_kv, 0)
    kv_loc[0, own_rows(h), :] = k_ref[:, head_columns(h, SPAN)]
    kv_loc[1, own_rows(h), :] = v_ref[:, head_columns(h, SPAN)]
    if nh > 1:
        await_bytes(kv_loc.at[:, pl.ds(0, (nh - 1) * rows), :], recv_sem.at[0])

    for kind in range(2):
        whole = kv_loc[kind].astype(f32)
        for piece in range(PIECES):
            upper = whole[piece * 8 : piece * 8 + 8]
            lower = whole[BLOCK + piece * 8 : BLOCK + piece * 8 + 8]
            spread[kind * PIECES + piece] = jnp.concatenate([upper, lower], axis=0).astype(bf16)

    def send_spread(d, _):
        j = lax.rem(c + d, nc)
        remote(spread.at[rank_of(j)], r1.at[c], 1, {"ctx": j}).start()
        return 0

    lax.fori_loop(1, nc, send_spread, 0)
    r1[c] = spread[rank_of(c)]

    def send_q(d, _):
        g = lax.rem(h + d, nh)
        remote(q_ref.at[:, head_columns(g, wide)], q_loc.at[own_rows(h), :], 2, {"head": g}).start()
        return 0

    lax.fori_loop(1, nh, send_q, 0)
    q_loc[own_rows(h), :] = q_ref[:, head_columns(h, wide)]

    lane = lax.broadcasted_iota(jnp.int32, (SPAN, SPAN), 1)
    diagonal = lane == lax.broadcasted_iota(jnp.int32, (SPAN, SPAN), 0)
    first_half = lane[:1] < BLOCK
    b0, b1 = order[2 * c], order[2 * c + 1]
    line0 = seg_ref[pl.ds(b0 // 2, 1), :]
    line1 = seg_ref[pl.ds(b1 // 2, 1), :]
    line0 = jnp.where(lax.rem(b0, 2) == 0, line0, jnp.concatenate([line0[:, BLOCK:], line0[:, :BLOCK]], axis=1))
    line1 = jnp.where(lax.rem(b1, 2) == 1, line1, jnp.concatenate([line1[:, BLOCK:], line1[:, :BLOCK]], axis=1))
    label_row = jnp.where(first_half, line0, line1)
    label_col = jnp.sum(jnp.where(diagonal, label_row, 0), axis=1, keepdims=True)

    def count_lower(r, count):
        return count + jnp.where(seg_ref[pl.ds(r, 1), :] < label_col, 1, 0)

    count = lax.fori_loop(0, nc, count_lower, jnp.zeros((SPAN, SPAN), jnp.int32))
    start_col = jnp.sum(count, axis=1, keepdims=True)
    start_row = jnp.sum(jnp.where(diagonal, start_col, 0), axis=0, keepdims=True)
    swapped = jnp.concatenate([start_row[:, BLOCK:], start_row[:, :BLOCK]], axis=1)
    shape4 = (PIECES, SEEN, 8, SPAN)
    key_place = (
        lax.broadcasted_iota(jnp.int32, shape4, 0) * 8
        + lax.broadcasted_iota(jnp.int32, shape4, 1) * BLOCK
        + lax.broadcasted_iota(jnp.int32, shape4, 2)
    ).reshape(WINDOW, SPAN)
    high = BACK * BLOCK + jnp.where(first_half, lane[:1], lane[:1] - BLOCK)
    for i, b in enumerate((b0, b1)):
        both = jnp.where(first_half, start_row, swapped) if i == 0 else jnp.where(first_half, swapped, start_row)
        low = both - (b - BACK) * BLOCK
        bias[i] = jnp.where((key_place >= low) & (key_place <= high), 0.0, NEVER)

    for i in range(2):
        for head in range(GROUP):
            part = do_ref[i * BLOCK : (i + 1) * BLOCK, head * SPAN : (head + 1) * SPAN].astype(f32)
            dot_t[i, :, head * BLOCK : (head + 1) * BLOCK] = part.T

    await_bytes(r1.at[pl.ds(0, nc - 1)], recv_sem.at[1])
    stored[...] = r1[...].astype(f32).reshape(blocks, 8, SPAN)
    seq[pl.ds(0, BACK)] = jnp.zeros((BACK, 8, SPAN), f32)

    def to_sequence(b, _):
        seq[b + BACK] = stored[place[b]]
        return 0

    lax.fori_loop(0, blocks, to_sequence, 0, unroll=8)

    def windows_of(j):
        both = [seq[pl.ds(order[2 * j + i], SEEN)] for i in range(2)]
        return jnp.concatenate(both, axis=0).reshape(2 * PART, SPAN).astype(bf16)

    def send_windows(e, _):
        j = member(c, e)
        s2[e] = windows_of(j)
        remote(s2.at[e], r2.at[rank_of(c)], 3, {"ctx": j}).start()
        return 0

    lax.fori_loop(1, CLASSES, send_windows, 0)
    r2[rank_of(c)] = windows_of(c)
    await_bytes(r2.at[pl.ds(0, CLASSES - 1)], recv_sem.at[3])
    for kind, target in enumerate((keys, vals)):
        for i in range(2):
            for piece in range(PIECES):
                both = r2[kind * PIECES + piece].astype(f32)
                target[i, piece * PART : (piece + 1) * PART, :] = both[i * PART : (i + 1) * PART]
    if nh > 1:
        await_bytes(q_loc.at[pl.ds(0, (nh - 1) * rows), :], recv_sem.at[2])

    scale = SPAN ** (-0.5)
    power = scale * float(np.log2(np.e))
    key_grads, value_grads = [], []
    for i in range(2):
        key_tile, value_tile = keys[i].astype(bf16), vals[i].astype(bf16)
        block = pl.ds(i * BLOCK, BLOCK)
        for part in range(GROUP * BLOCK // LANES):
            heads = range(part * LANES // BLOCK, (part + 1) * LANES // BLOCK)
            lanes = slice(part * LANES, (part + 1) * LANES)
            query = jnp.concatenate([q_loc[block, a * SPAN : (a + 1) * SPAN] for a in heads], axis=0)
            cotangent = jnp.concatenate([do_ref[block, a * SPAN : (a + 1) * SPAN] for a in heads], axis=0)
            scores = lax.dot_general(key_tile, query, NT, preferred_element_type=f32)
            scores = scores + jnp.concatenate([bias[i]] * (LANES // SPAN), axis=1)
            top = jnp.max(scores, axis=0, keepdims=True)
            raised = jnp.exp2((scores - top) * power)
            total = jnp.sum(raised, axis=0, keepdims=True)
            sums = lax.dot_general(value_tile, raised.astype(bf16), TN, preferred_element_type=f32)
            inverse = 1.0 / total
            attended = (sums * inverse).astype(bf16).astype(f32)
            dsum = jnp.sum(dot_t[i, :, lanes] * attended, axis=0, keepdims=True)
            prob = raised * inverse
            probs[:, lanes] = prob.astype(bf16)
            dprob = lax.dot_general(value_tile, cotangent, NT, preferred_element_type=f32)
            dscore = (prob * (dprob - dsum)).astype(bf16)
            dscores[:, lanes] = dscore
            query_grad = lax.dot_general(key_tile, dscore, TN, preferred_element_type=f32) * scale
            attended_rows = attended.T.astype(bf16)
            query_grad_rows = query_grad.T.astype(bf16)
            for n, a in enumerate(heads):
                att_out[block, a * SPAN : (a + 1) * SPAN] = attended_rows[n * BLOCK : (n + 1) * BLOCK]
                dq_loc[block, a * SPAN : (a + 1) * SPAN] = query_grad_rows[n * BLOCK : (n + 1) * BLOCK]
        query = jnp.concatenate([q_loc[block, a * SPAN : (a + 1) * SPAN] for a in range(GROUP)], axis=0)
        cotangent = jnp.concatenate([do_ref[block, a * SPAN : (a + 1) * SPAN] for a in range(GROUP)], axis=0)
        keys[i] = jnp.dot(dscores[...], query, preferred_element_type=f32) * scale
        vals[i] = jnp.dot(probs[...], cotangent, preferred_element_type=f32)

    for kind, source in enumerate((keys, vals)):
        for piece in range(PIECES):
            both = [source[i, piece * PART : (piece + 1) * PART, :] for i in range(2)]
            s3[kind * PIECES + piece] = jnp.concatenate(both, axis=0).astype(bf16)

    def send_back(e, _):
        j = member(c, e)
        remote(s3.at[rank_of(j)], r3.at[rank_of(c)], 4, {"ctx": j}).start()
        return 0

    lax.fori_loop(1, CLASSES, send_back, 0)
    r3[rank_of(c)] = s3[rank_of(c)]

    def send_dq(d, _):
        g = lax.rem(h + d, nh)
        remote(dq_loc.at[own_rows(g), :], dq_out.at[:, head_columns(h, wide)], 5, {"head": g}).start()
        return 0

    lax.fori_loop(1, nh, send_dq, 0)
    dq_out[:, head_columns(h, wide)] = dq_loc[own_rows(h), :]

    await_bytes(r3.at[pl.ds(0, CLASSES - 1)], recv_sem.at[4])
    r3f[pl.ds(0, 2 * CLASSES)] = r3[...].astype(f32).reshape(2 * CLASSES, SEEN, 8, SPAN)
    r3f[2 * CLASSES] = jnp.zeros((SEEN, 8, SPAN), f32)

    def add_up(b, sums):
        s = place[b]
        j = s // 2
        slot = jnp.where(j // CLASSES == c // CLASSES, rank_of(j) * 2 + lax.rem(s, 2), 2 * CLASSES)
        new = r3f[slot]
        sums = [sums[k] + new[k] for k in range(SEEN)]
        acc[b] = sums[0]
        return tuple(sums[1:]) + (jnp.zeros((8, SPAN), f32),)

    sums = lax.fori_loop(0, blocks, add_up, tuple(jnp.zeros((8, SPAN), f32) for _ in range(SEEN)), unroll=4)
    for k in range(BACK):
        acc[blocks + k] = sums[k]

    def tile_of(j):
        both = [acc[order[2 * j + i] + BACK] for i in range(2)]
        return jnp.concatenate(both, axis=0).astype(bf16)

    def send_sums(d, _):
        j = lax.rem(c + d, nc)
        s4[j] = tile_of(j)
        remote(s4.at[j], r4.at[c], 6, {"ctx": j}).start()
        return 0

    lax.fori_loop(1, nc, send_sums, 0)
    r4[c] = tile_of(c)
    await_bytes(r4.at[pl.ds(0, nc - 1)], recv_sem.at[6])
    for kind in range(2):
        uppers, lowers = [], []
        for piece in range(PIECES):
            base = (piece // LINE) * LINE * PAIR + kind * LINE + piece % LINE
            tile = r4[base].astype(f32)
            for copy in range(1, nc // CLASSES):
                tile = tile + r4[copy * CLASSES + base].astype(f32)
            uppers.append(tile[:8])
            lowers.append(tile[8:])
        dkv_loc[kind] = jnp.concatenate(uppers + lowers, axis=0).astype(bf16)

    def send_dkv(d, _):
        g = lax.rem(h + d, nh)
        remote(dkv_loc.at[0, own_rows(g), :], dk_out.at[:, head_columns(h, SPAN)], 7, {"head": g}).start()
        remote(dkv_loc.at[1, own_rows(g), :], dv_out.at[:, head_columns(h, SPAN)], 7, {"head": g}).start()
        return 0

    lax.fori_loop(1, nh, send_dkv, 0)
    dk_out[:, head_columns(h, SPAN)] = dkv_loc[0, own_rows(h), :]
    dv_out[:, head_columns(h, SPAN)] = dkv_loc[1, own_rows(h), :]

    some = pl.ds(0, (nh - 1) * rows)
    if nh > 1:
        await_bytes(q_loc.at[some, :], recv_sem.at[5])
        await_bytes(kv_loc.at[:, some, :], recv_sem.at[7])
        await_bytes(kv_loc.at[:, some, :], send_sem.at[0])
        await_bytes(q_loc.at[some, :], send_sem.at[2])
        await_bytes(q_loc.at[some, :], send_sem.at[5])
        await_bytes(kv_loc.at[:, some, :], send_sem.at[7])
    await_bytes(r1.at[pl.ds(0, nc - 1)], send_sem.at[1])
    await_bytes(r2.at[pl.ds(0, CLASSES - 1)], send_sem.at[3])
    await_bytes(r3.at[pl.ds(0, CLASSES - 1)], send_sem.at[4])
    await_bytes(r4.at[pl.ds(0, nc - 1)], send_sem.at[6])


def shards(queries, keys, values, output_gradient, segment_ids, block_order):
    nc, nh = lax.axis_size("ctx"), lax.axis_size("head")
    rows, wide, blocks = queries.shape[0], GROUP * SPAN, 2 * nc
    spots = jnp.arange(blocks, dtype=jnp.int32)
    place = jnp.sum(jnp.where(block_order[None, :] == spots[:, None], spots[None, :], 0), axis=1, dtype=jnp.int32)
    bf16, f32 = jnp.bfloat16, jnp.float32
    vmem = pl.BlockSpec(memory_space=pltpu.VMEM)
    smem = pl.BlockSpec(memory_space=pltpu.SMEM)
    return pl.pallas_call(
        functools.partial(kernel, nc, nh),
        out_shape=(
            jax.ShapeDtypeStruct((2 * BLOCK, wide), bf16),
            jax.ShapeDtypeStruct(queries.shape, bf16),
            jax.ShapeDtypeStruct(keys.shape, bf16),
            jax.ShapeDtypeStruct(values.shape, bf16),
        ),
        in_specs=[smem, smem, vmem, vmem, vmem, vmem, vmem],
        out_specs=(vmem, vmem, vmem, vmem),
        scratch_shapes=[
            pltpu.VMEM((2 * BLOCK, wide), bf16),
            pltpu.VMEM((2, 2 * BLOCK, SPAN), bf16),
            pltpu.VMEM((CLASSES, 16, SPAN), bf16),
            pltpu.VMEM((nc, 16, SPAN), bf16),
            pltpu.VMEM((blocks, 8, SPAN), f32),
            pltpu.VMEM((blocks + BACK, 8, SPAN), f32),
            pltpu.VMEM((CLASSES, 2 * PART, SPAN), bf16),
            pltpu.VMEM((CLASSES, 2 * PART, SPAN), bf16),
            pltpu.VMEM((2, WINDOW, SPAN), f32),
            pltpu.VMEM((2, WINDOW, SPAN), f32),
            pltpu.VMEM((2, SPAN, GROUP * BLOCK), f32),
            pltpu.VMEM((2, WINDOW, SPAN), f32),
            pltpu.VMEM((WINDOW, GROUP * BLOCK), bf16),
            pltpu.VMEM((WINDOW, GROUP * BLOCK), bf16),
            pltpu.VMEM((2 * BLOCK, wide), bf16),
            pltpu.VMEM((CLASSES, 2 * PART, SPAN), bf16),
            pltpu.VMEM((CLASSES, 2 * PART, SPAN), bf16),
            pltpu.VMEM((2 * CLASSES + 1, SEEN, 8, SPAN), f32),
            pltpu.VMEM((blocks + BACK, 8, SPAN), f32),
            pltpu.VMEM((nc, 16, SPAN), bf16),
            pltpu.VMEM((nc, 16, SPAN), bf16),
            pltpu.VMEM((2, 2 * BLOCK, SPAN), bf16),
            pltpu.SemaphoreType.DMA((8,)),
            pltpu.SemaphoreType.DMA((8,)),
        ],
        compiler_params=pltpu.CompilerParams(
            collective_id=0, has_side_effects=True, vmem_limit_bytes=48 * 1024 * 1024
        ),
    )(block_order, place, queries, keys, values, output_gradient, segment_ids.reshape(nc, 2 * BLOCK))


def solution(mesh):
    in_specs = (
        P(("ctx", "head"), None),
        P(("ctx", "head"), None),
        P(("ctx", "head"), None),
        P("ctx", "head"),
        P(),
        P(),
    )
    out_specs = (
        P("ctx", "head"),
        P(("ctx", "head"), None),
        P(("ctx", "head"), None),
        P(("ctx", "head"), None),
    )
    return jax.shard_map(shards, mesh=mesh, in_specs=in_specs, out_specs=out_specs, check_vma=False)
```

time: 1760 us -> 82.5 us (0.05); the launches traced: 1740 us -> 82.1 us
  waiting for transfers between devices: 694 us -> 0 us
  loops' own time: 279 us -> 0 us
  starting transfers between devices: 277 us -> 0 us
  local copies, waits for them, and re-layouts: 192 us -> 7.46 us
  blocking collectives: 156 us -> 0 us
  other arithmetic: 121 us -> 0.1 us
  Pallas kernels: 0 us -> 73.8 us
    ppermute x127 -> x0, waiting for transfers between devices: 664 us -> none  [from_behind(): lax.ppermute(x, axis, [(i, (i + by) % length) for i in range(length)])]
    another operation x130 -> x0, loops' own time: 279 us -> none  [the longest x1 132 us: shards(): lax.fori_loop(0, cycle_size, backward_step, start_grads)]
    ppermute x127 -> x0, starting transfers between devices: 246 us -> none  [from_behind(): lax.ppermute(x, axis, [(i, (i + by) % length) for i in range(length)])]
    dynamic_slice x256 -> x0, local copies, waits for them, and re-layouts: 177 us -> none  [the longest x128 101 us: block_places(): lax.dynamic_slice_in_dim(segment_ids, start_upper, HALF)]
    all_to_all x1 -> x0, blocking collectives: 156 us -> none  [shards(): lax.all_to_all(value_gradient, 'head', split_axis=0, concat_axis=1, tiled...]
    reduce_or x128 -> x0, other arithmetic: 87.8 us -> none  [the longest x64 47.2 us: cycle_visit(): return lax.cond(jnp.any(allowed), take, lambda inner: inner, (soft, store))]
    pallas_call x0 -> x1, Pallas kernels: none -> 73.8 us  [shards(): pl.pallas_call(functools.partial(kernel, nc, nh), out_shape=(jax.ShapeDty...]
    all_to_all x5 -> x0, starting transfers between devices: 31.8 us -> none  [the longest x1 11.8 us: shards(): lax.all_to_all(keys, 'head', split_axis=1, concat_axis=0, tiled=True)]
  transfers between devices with their start and end apart: 132 -> 0, of which waited for: 132 -> 0; matrix products, arithmetic and copies ran while one was open for 9% -> 0% of each run, Pallas kernels for 0% -> 0%
where the time goes in v1:
time: 82.5 us; the launch traced here: 82.1 us
  Pallas kernels  73.8 us (89%)
  local copies, waits for them, and re-layouts  7.46 us (9%)
    pallas_call x1, Pallas kernels, shards(): pl.pallas_call(functools.partial(kernel, nc, nh), out_shape=(jax.ShapeDty...  73.8 us
    unnamed x16, local copies, waits for them, and re-layouts  7.46 us

profile of v1, /device:TPU:1, one launch (start us, length us, event | category | flops | bytes accessed | tf_op | source)
XLA Modules:
  0.0 82.1 jit_solution(2242308435532987526)
XLA Ops:
  0.6 0.0 copy-start.5
  0.6 0.6 copy-done.5
  1.3 0.1 select_reduce_fusion.place
  1.4 0.0 copy-start
  1.4 0.9 %copy-done = bf16[16,8192]{1,0:T(8,128)(2,1)S(1)} copy-done((bf16[16,8192]{1,0:T(8,128)(2,1)S(1)}, bf16[16,8192]{1,0:T(8,128)(2,1)}, u32[]{:S(2)}) %copy-start) | copy-done | bytes 262168
  2.4 0.0 copy-start.1
  2.4 0.9 %copy-done.1 = bf16[128,1024]{1,0:T(8,128)(2,1)S(1)} copy-done((bf16[128,1024]{1,0:T(8,128)(2,1)S(1)}, bf16[128,1024]{1,0:T(8,128)(2,1)}, u32[]{:S(2)}) %copy-start.1) | copy-done | bytes 262168
  3.3 0.0 copy-start.2
  3.3 0.8 copy-done.2
  4.1 0.0 copy-start.3
  4.1 0.8 copy-done.3
  4.8 0.0 copy-start.4
  4.8 0.8 copy-done.4
  5.6 73.8 %shard_map.93 = (bf16[128,1024]{1,0:T(8,128)(2,1)S(1)}, bf16[16,8192]{1,0:T(8,128)(2,1)S(1)}, bf16[16,1024]{1,0:T(8,128)(2,1)S(1)}, bf16[16,1024]{1,0:T(8,128)(2,1)S(1)}) custom-call(s32[128]{0:T(128)S(1)} %copy-done.5, s32[128]{0:T(128)S(1)} %select_reduce_fusion.place, bf16[16,8192]{1,0:T(8,128)(2,1)S(1)} %copy-done, bf16[16,1024]{1,0:T(8,128)(2,1)S(1)} %copy-done.2, ...), custom_call_target="tpu_custom_call" | custom-call | tf_op jit(solution)/shard_map/pallas_call | solution.py:317
  79.4 0.7 copy.14
  80.1 0.7 copy.15
  80.8 0.6 copy.16
  81.4 0.6 copy.17
Async XLA Ops:
  0.6 0.7 copy-start.5
  1.4 1.0 %copy-start = (bf16[16,8192]{1,0:T(8,128)(2,1)S(1)}, bf16[16,8192]{1,0:T(8,128)(2,1)}, u32[]{:S(2)}) copy-start(bf16[16,8192]{1,0:T(8,128)(2,1)} %q_ref.1) | copy-start | bytes 786436
  2.4 0.9 %copy-start.1 = (bf16[128,1024]{1,0:T(8,128)(2,1)S(1)}, bf16[128,1024]{1,0:T(8,128)(2,1)}, u32[]{:S(2)}) copy-start(bf16[128,1024]{1,0:T(8,128)(2,1)} %do_ref.1) | copy-start | bytes 786436
  3.3 0.8 copy-start.2
  4.1 0.8 copy-start.3
  4.8 0.8 copy-start.4

commit v2 on v1

--- a/solution.py
+++ b/solution.py
@@ -44,11 +44,12 @@
 
 def kernel(
     nc, nh,
-    order, place, q_ref, k_ref, v_ref, do_ref, seg_ref,
+    order_hbm, q_ref, k_ref, v_ref, do_hbm, seg_hbm,
     att_out, dq_out, dk_out, dv_out,
     q_loc, kv_loc, spread, r1, stored, seq, s2, r2, keys, vals, dot_t, bias,
     probs, dscores, dq_loc, s3, r3, r3f, acc, s4, r4, dkv_loc,
-    send_sem, recv_sem,
+    do_ref, seg_ref, order_row, place_row, order, place,
+    send_sem, recv_sem, local_sem,
 ):
     c = lax.axis_index("ctx")
     h = lax.axis_index("head")
@@ -75,13 +76,39 @@
 
     lax.fori_loop(1, nh, greet_head, 0)
     lax.fori_loop(1, nc, greet_ctx, 0)
-    pl.semaphore_wait(barrier, nc - 1 + nh - 1)
 
     def own_rows(g):
         return pl.ds(pl.multiple_of(g * rows, rows), rows)
 
     def head_columns(g, width):
         return pl.ds(pl.multiple_of(g * width, width), width)
+
+    fetch_kv = [
+        pltpu.make_async_copy(source.at[:, head_columns(h, SPAN)], kv_loc.at[kind, own_rows(h), :], local_sem.at[kind])
+        for kind, source in enumerate((k_ref, v_ref))
+    ]
+    fetch_order = [
+        pltpu.make_async_copy(order_hbm, order, local_sem.at[2]),
+        pltpu.make_async_copy(order_hbm, order_row, local_sem.at[3]),
+    ]
+    fetch_rest = [
+        pltpu.make_async_copy(seg_hbm, seg_ref, local_sem.at[4]),
+        pltpu.make_async_copy(do_hbm, do_ref, local_sem.at[5]),
+        pltpu.make_async_copy(q_ref.at[:, head_columns(h, wide)], q_loc.at[own_rows(h), :], local_sem.at[6]),
+    ]
+    for fetch in fetch_order + fetch_kv + fetch_rest:
+        fetch.start()
+    for fetch in fetch_order:
+        fetch.wait()
+
+    spot = lax.broadcasted_iota(jnp.int32, (blocks, blocks), 0)
+    across = lax.broadcasted_iota(jnp.int32, (blocks, blocks), 1)
+    order_col = jnp.sum(jnp.where(spot == across, order_row[...], 0), axis=1, keepdims=True)
+    place_row[...] = jnp.max(jnp.where(order_col == across, spot, 0), axis=0, keepdims=True)
+    fetch_place = pltpu.make_async_copy(place_row, place, local_sem.at[7])
+    fetch_place.start()
+
+    pl.semaphore_wait(barrier, nc - 1 + nh - 1)
 
     def send_kv(d, _):
         g = lax.rem(h + d, nh)
@@ -90,8 +117,8 @@
         return 0
 
     lax.fori_loop(1, nh, send_kv, 0)
-    kv_loc[0, own_rows(h), :] = k_ref[:, head_columns(h, SPAN)]
-    kv_loc[1, own_rows(h), :] = v_ref[:, head_columns(h, SPAN)]
+    for fetch in fetch_kv:
+        fetch.wait()
     if nh > 1:
         await_bytes(kv_loc.at[:, pl.ds(0, (nh - 1) * rows), :], recv_sem.at[0])
 
@@ -116,12 +143,14 @@
         return 0
 
     lax.fori_loop(1, nh, send_q, 0)
-    q_loc[own_rows(h), :] = q_ref[:, head_columns(h, wide)]
+    for fetch in fetch_rest:
+        fetch.wait()
+    fetch_place.wait()
 
     lane = lax.broadcasted_iota(jnp.int32, (SPAN, SPAN), 1)
     diagonal = lane == lax.broadcasted_iota(jnp.int32, (SPAN, SPAN), 0)
     first_half = lane[:1] < BLOCK
-    b0, b1 = order[2 * c], order[2 * c + 1]
+    b0, b1 = order[0, 2 * c], order[0, 2 * c + 1]
     line0 = seg_ref[pl.ds(b0 // 2, 1), :]
     line1 = seg_ref[pl.ds(b1 // 2, 1), :]
     line0 = jnp.where(lax.rem(b0, 2) == 0, line0, jnp.concatenate([line0[:, BLOCK:], line0[:, :BLOCK]], axis=1))
@@ -158,13 +187,13 @@
     seq[pl.ds(0, BACK)] = jnp.zeros((BACK, 8, SPAN), f32)
 
     def to_sequence(b, _):
-        seq[b + BACK] = stored[place[b]]
+        seq[b + BACK] = stored[place[0, b]]
         return 0
 
     lax.fori_loop(0, blocks, to_sequence, 0, unroll=8)
 
     def windows_of(j):
-        both = [seq[pl.ds(order[2 * j + i], SEEN)] for i in range(2)]
+        both = [seq[pl.ds(order[0, 2 * j + i], SEEN)] for i in range(2)]
         return jnp.concatenate(both, axis=0).reshape(2 * PART, SPAN).astype(bf16)
 
     def send_windows(e, _):
@@ -233,20 +262,12 @@
     lax.fori_loop(1, CLASSES, send_back, 0)
     r3[rank_of(c)] = s3[rank_of(c)]
 
-    def send_dq(d, _):
-        g = lax.rem(h + d, nh)
-        remote(dq_loc.at[own_rows(g), :], dq_out.at[:, head_columns(h, wide)], 5, {"head": g}).start()
-        return 0
-
-    lax.fori_loop(1, nh, send_dq, 0)
-    dq_out[:, head_columns(h, wide)] = dq_loc[own_rows(h), :]
-
     await_bytes(r3.at[pl.ds(0, CLASSES - 1)], recv_sem.at[4])
     r3f[pl.ds(0, 2 * CLASSES)] = r3[...].astype(f32).reshape(2 * CLASSES, SEEN, 8, SPAN)
     r3f[2 * CLASSES] = jnp.zeros((SEEN, 8, SPAN), f32)
 
     def add_up(b, sums):
-        s = place[b]
+        s = place[0, b]
         j = s // 2
         slot = jnp.where(j // CLASSES == c // CLASSES, rank_of(j) * 2 + lax.rem(s, 2), 2 * CLASSES)
         new = r3f[slot]
@@ -259,7 +280,7 @@
         acc[blocks + k] = sums[k]
 
     def tile_of(j):
-        both = [acc[order[2 * j + i] + BACK] for i in range(2)]
+        both = [acc[order[0, 2 * j + i] + BACK] for i in range(2)]
         return jnp.concatenate(both, axis=0).astype(bf16)
 
     def send_sums(d, _):
@@ -270,6 +291,15 @@
 
     lax.fori_loop(1, nc, send_sums, 0)
     r4[c] = tile_of(c)
+
+    def send_dq(d, _):
+        g = lax.rem(h + d, nh)
+        remote(dq_loc.at[own_rows(g), :], dq_out.at[:, head_columns(h, wide)], 5, {"head": g}).start()
+        return 0
+
+    lax.fori_loop(1, nh, send_dq, 0)
+    dq_out[:, head_columns(h, wide)] = dq_loc[own_rows(h), :]
+
     await_bytes(r4.at[pl.ds(0, nc - 1)], recv_sem.at[6])
     for kind in range(2):
         uppers, lowers = [], []
@@ -309,20 +339,19 @@
 def shards(queries, keys, values, output_gradient, segment_ids, block_order):
     nc, nh = lax.axis_size("ctx"), lax.axis_size("head")
     rows, wide, blocks = queries.shape[0], GROUP * SPAN, 2 * nc
-    spots = jnp.arange(blocks, dtype=jnp.int32)
-    place = jnp.sum(jnp.where(block_order[None, :] == spots[:, None], spots[None, :], 0), axis=1, dtype=jnp.int32)
-    bf16, f32 = jnp.bfloat16, jnp.float32
+    bf16, f32, i32 = jnp.bfloat16, jnp.float32, jnp.int32
     vmem = pl.BlockSpec(memory_space=pltpu.VMEM)
-    smem = pl.BlockSpec(memory_space=pltpu.SMEM)
+    anywhere = pl.BlockSpec(memory_space=pl.ANY)
+    shapes = (
+        jax.ShapeDtypeStruct((2 * BLOCK, wide), bf16),
+        jax.ShapeDtypeStruct(queries.shape, bf16),
+        jax.ShapeDtypeStruct(keys.shape, bf16),
+        jax.ShapeDtypeStruct(values.shape, bf16),
+    )
     return pl.pallas_call(
         functools.partial(kernel, nc, nh),
-        out_shape=(
-            jax.ShapeDtypeStruct((2 * BLOCK, wide), bf16),
-            jax.ShapeDtypeStruct(queries.shape, bf16),
-            jax.ShapeDtypeStruct(keys.shape, bf16),
-            jax.ShapeDtypeStruct(values.shape, bf16),
-        ),
-        in_specs=[smem, smem, vmem, vmem, vmem, vmem, vmem],
+        out_shape=shapes,
+        in_specs=[anywhere] * 6,
         out_specs=(vmem, vmem, vmem, vmem),
         scratch_shapes=[
             pltpu.VMEM((2 * BLOCK, wide), bf16),
@@ -347,13 +376,20 @@
             pltpu.VMEM((nc, 16, SPAN), bf16),
             pltpu.VMEM((nc, 16, SPAN), bf16),
             pltpu.VMEM((2, 2 * BLOCK, SPAN), bf16),
+            pltpu.VMEM((2 * BLOCK, wide), bf16),
+            pltpu.VMEM((nc, 2 * BLOCK), i32),
+            pltpu.VMEM((1, blocks), i32),
+            pltpu.VMEM((1, blocks), i32),
+            pltpu.SMEM((1, blocks), i32),
+            pltpu.SMEM((1, blocks), i32),
+            pltpu.SemaphoreType.DMA((8,)),
             pltpu.SemaphoreType.DMA((8,)),
             pltpu.SemaphoreType.DMA((8,)),
         ],
         compiler_params=pltpu.CompilerParams(
-            collective_id=0, has_side_effects=True, vmem_limit_bytes=48 * 1024 * 1024
+            collective_id=0, has_side_effects=True, vmem_limit_bytes=63 * 1024 * 1024
         ),
-    )(block_order, place, queries, keys, values, output_gradient, segment_ids.reshape(nc, 2 * BLOCK))
+    )(block_order.reshape(1, blocks), queries, keys, values, output_gradient, segment_ids.reshape(nc, 2 * BLOCK))
 
 
 def solution(mesh):

time: 82.5 us -> 77.8 us (0.943)
  local copies, waits for them, and re-layouts: 7.46 us -> 3.86 us
    unnamed x16 -> x10, local copies, waits for them, and re-layouts: 7.46 us -> 3.86 us
where the time goes in v2:
time: 77.8 us; the launch traced here: 77.5 us
  Pallas kernels  73 us (94%)
  local copies, waits for them, and re-layouts  3.86 us (5%)
    pallas_call x1, Pallas kernels, shards(): pl.pallas_call(functools.partial(kernel, nc, nh), out_shape=shapes, in_sp...  73 us
    unnamed x10, local copies, waits for them, and re-layouts  3.86 us

profile of v2, /device:TPU:1, one launch (start us, length us, event | category | flops | bytes accessed | tf_op | source)
XLA Modules:
  0.0 77.5 jit_solution(5478145044886120811)
XLA Ops:
  0.6 73.0 %shard_map.93 = (bf16[128,1024]{1,0:T(8,128)(2,1)}, bf16[16,8192]{1,0:T(8,128)(2,1)}, bf16[16,1024]{1,0:T(8,128)(2,1)}, bf16[16,1024]{1,0:T(8,128)(2,1)}) custom-call(s32[1,128]{1,0:T(1,128)} %bitcast.3, bf16[16,8192]{1,0:T(8,128)(2,1)} %q_ref.1, bf16[16,1024]{1,0:T(8,128)(2,1)} %k_ref.1, bf16[16,1024]{1,0:T(8,128)(2,1)} %v_ref.1, bf16[128,1024]{1,0:T(8,128)(2,1)} %do_hbm.1, ...), custom_call_target="tpu_custom_call" | custom-call | tf_op jit(solution)/shard_map/pallas_call | solution.py:351
  73.7 0.0 copy-start
  73.7 1.7 %copy.14 = bf16[128,1024]{1,0:T(8,128)(2,1)} copy(bf16[128,1024]{1,0:T(8,128)(2,1)} %get-tuple-element.8) | data formatting | bytes 524288
  75.4 0.0 copy-done
  75.4 0.0 copy-start.2
  75.4 0.7 copy.15
  76.1 0.1 copy-done.2
  76.1 0.0 copy-start.1
  76.1 0.6 copy.16
  76.8 0.2 copy-done.1
  76.9 0.6 copy.17
Async XLA Ops:
  73.7 1.7 %copy-start = (bf16[16,8192]{1,0:T(8,128)(2,1)S(1)}, bf16[16,8192]{1,0:T(8,128)(2,1)}, u32[]{:S(2)}) copy-start(bf16[16,8192]{1,0:T(8,128)(2,1)} %get-tuple-element.9) | copy-start | bytes 786436
  75.4 0.8 copy-start.2
  76.1 0.8 copy-start.1

commit v3 on v2

v3 whole, which is shorter than its diff:
```python
import functools

import jax
import jax.numpy as jnp
import numpy as np
from jax import lax
from jax.experimental import pallas as pl
from jax.experimental.pallas import tpu as pltpu
from jax.sharding import PartitionSpec as P

SPAN = 128
BLOCK = 64
GROUP = 8
BACK = 8
SEEN = BACK + 1
WINDOW = SEEN * BLOCK
LINE = 4
PAIR = 2
PLANE = LINE * PAIR
HEADS = 8
CLASSES = 16
PIECES = 8
PART = SEEN * 8
LANES = 256
NEVER = -1e30

MESH = pl.DeviceIdType.MESH
NT = (((1,), (1,)), ((), ()))
TN = (((0,), (0,)), ((), ()))


def rank_of(c):
    return lax.rem(c // LINE, PAIR) * PIECES + lax.rem(c, LINE) * 2 + lax.rem(c // PLANE, 2)


def member(c, e):
    x = lax.rem(lax.rem(c, LINE) + lax.rem(e, LINE), LINE)
    z = lax.rem(lax.rem(c // LINE, PAIR) + lax.rem(e // LINE, PAIR), PAIR)
    y = lax.rem(lax.rem(c // PLANE, 2) + e // PLANE, 2)
    return (c // CLASSES) * CLASSES + (y * PAIR + z) * LINE + x


def await_bytes(ref, sem):
    pltpu.make_async_copy(ref, ref, sem).wait()


def kernel(
    nc,
    order_hbm, q_ref, k_ref, v_ref, do_hbm, seg_hbm,
    att_out, dq_out, dk_out, dv_out,
    q_loc, dealt, spread, r1, stored, seq, s2, r2, keys, vals, dot_t, bias,
    probs, dscores, dq_loc, s3, r3, r3f, acc, s4, r4, summed,
    do_ref, seg_ref, order_row, place_row, order, place,
    send_sem, recv_sem, local_sem,
):
    c = lax.axis_index("ctx")
    h = lax.axis_index("head")
    y, z, x, zx = c // PLANE, lax.rem(c // LINE, PAIR), lax.rem(c, LINE), lax.rem(c, PLANE)
    ny = nc // PLANE
    rows = q_ref.shape[0]
    wide = GROUP * SPAN
    blocks = 2 * nc
    f32, bf16 = jnp.float32, jnp.bfloat16
    own_deal = x == lax.rem(h, LINE)

    def remote(src, dst, which, where):
        return pltpu.make_async_remote_copy(
            src_ref=src, dst_ref=dst, send_sem=send_sem.at[which], recv_sem=recv_sem.at[which],
            device_id=where, device_id_type=MESH,
        )

    def for_each(low, high, what):
        def step(d, _):
            what(d)
            return 0

        lax.fori_loop(low, high, step, 0)

    barrier = pltpu.get_barrier_semaphore()

    def greet(where):
        pl.semaphore_signal(barrier, inc=1, device_id=where, device_id_type=MESH)

    def greet_dealer(d):
        greet({"ctx": y * PLANE + lax.rem(zx + d // 2, PLANE), "head": x + LINE * lax.rem(d, 2)})

    for_each(2, 2 * PLANE, greet_dealer)
    for half in range(2):

        @pl.when(x + LINE * half != h)
        def _():
            greet({"ctx": c, "head": x + LINE * half})

    for_each(1, CLASSES, lambda e: greet({"ctx": member(c, e)}))
    for_each(1, ny, lambda d: greet({"ctx": lax.rem(c + d * PLANE, nc)}))
    for_each(1, HEADS, lambda d: greet({"head": lax.rem(h + d, HEADS)}))

    def own_rows(g):
        return pl.ds(pl.multiple_of(g * rows, rows), rows)

    def head_columns(g, width):
        return pl.ds(pl.multiple_of(g * width, width), width)

    fetch_order = [
        pltpu.make_async_copy(order_hbm, order, local_sem.at[2]),
        pltpu.make_async_copy(order_hbm, order_row, local_sem.at[3]),
    ]
    fetch_rest = [
        pltpu.make_async_copy(seg_hbm, seg_ref, local_sem.at[4]),
        pltpu.make_async_copy(do_hbm, do_ref, local_sem.at[5]),
        pltpu.make_async_copy(q_ref.at[:, head_columns(h, wide)], q_loc.at[own_rows(h), :], local_sem.at[6]),
    ]
    for fetch in fetch_order + fetch_rest:
        fetch.start()
    for fetch in fetch_order:
        fetch.wait()

    spot = lax.broadcasted_iota(jnp.int32, (blocks, blocks), 0)
    across = lax.broadcasted_iota(jnp.int32, (blocks, blocks), 1)
    order_col = jnp.sum(jnp.where(spot == across, order_row[...], 0), axis=1, keepdims=True)
    place_row[...] = jnp.max(jnp.where(order_col == across, spot, 0), axis=0, keepdims=True)
    fetch_place = pltpu.make_async_copy(place_row, place, local_sem.at[7])
    fetch_place.start()

    others = 2 * PLANE + CLASSES - 1 + ny - 1 + HEADS - 1

    @pl.when(own_deal)
    def _():
        pl.semaphore_wait(barrier, others - 1)

    @pl.when(jnp.logical_not(own_deal))
    def _():
        pl.semaphore_wait(barrier, others)

    slot = zx * 2 + h // LINE
    for kind, source in enumerate((k_ref, v_ref)):
        there = (y * PAIR + kind) * LINE + lax.rem(h, LINE)

        def deal(d):
            g = lax.rem(h + d, HEADS)
            remote(source.at[:, head_columns(g, SPAN)], dealt.at[slot], 0, {"ctx": there, "head": g}).start()

        for_each(1, HEADS, deal)
        stays = own_deal & (z == kind)

        @pl.when(jnp.logical_not(stays))
        def _():
            deal(0)

        @pl.when(stays)
        def _():
            pltpu.make_async_copy(source.at[:, head_columns(h, SPAN)], dealt.at[slot], recv_sem.at[0]).start()

    await_bytes(dealt, recv_sem.at[0])

    halves = dealt[...].astype(f32).reshape(PLANE, 2, 2, 8, SPAN)
    for half in range(2):
        spread[half] = halves[:, :, half].reshape(PLANE, 16, SPAN).astype(bf16)

    def own_plane(there):
        return pl.ds(there * PLANE, PLANE)

    def send_spread(d):
        there = lax.rem(y + d, ny)
        remote(spread.at[lax.rem(there, 2)], r1.at[own_plane(y)], 1, {"ctx": there * PLANE + zx}).start()

    for_each(1, ny, send_spread)
    r1[own_plane(y)] = spread[lax.rem(y, 2)]

    def send_q(d):
        g = lax.rem(h + d, HEADS)
        remote(q_ref.at[:, head_columns(g, wide)], q_loc.at[own_rows(h), :], 2, {"head": g}).start()

    for_each(1, HEADS, send_q)
    for fetch in fetch_rest:
        fetch.wait()
    fetch_place.wait()

    lane = lax.broadcasted_iota(jnp.int32, (SPAN, SPAN), 1)
    diagonal = lane == lax.broadcasted_iota(jnp.int32, (SPAN, SPAN), 0)
    first_half = lane[:1] < BLOCK
    b0, b1 = order[0, 2 * c], order[0, 2 * c + 1]
    line0 = seg_ref[pl.ds(b0 // 2, 1), :]
    line1 = seg_ref[pl.ds(b1 // 2, 1), :]
    line0 = jnp.where(lax.rem(b0, 2) == 0, line0, jnp.concatenate([line0[:, BLOCK:], line0[:, :BLOCK]], axis=1))
    line1 = jnp.where(lax.rem(b1, 2) == 1, line1, jnp.concatenate([line1[:, BLOCK:], line1[:, :BLOCK]], axis=1))
    label_row = jnp.where(first_half, line0, line1)
    label_col = jnp.sum(jnp.where(diagonal, label_row, 0), axis=1, keepdims=True)

    def count_lower(r, count):
        return count + jnp.where(seg_ref[pl.ds(r, 1), :] < label_col, 1, 0)

    count = lax.fori_loop(0, nc, count_lower, jnp.zeros((SPAN, SPAN), jnp.int32))
    start_col = jnp.sum(count, axis=1, keepdims=True)
    start_row = jnp.sum(jnp.where(diagonal, start_col, 0), axis=0, keepdims=True)
    swapped = jnp.concatenate([start_row[:, BLOCK:], start_row[:, :BLOCK]], axis=1)
    shape4 = (PIECES, SEEN, 8, SPAN)
    key_place = (
        lax.broadcasted_iota(jnp.int32, shape4, 0) * 8
        + lax.broadcasted_iota(jnp.int32, shape4, 1) * BLOCK
        + lax.broadcasted_iota(jnp.int32, shape4, 2)
    ).reshape(WINDOW, SPAN)
    high = BACK * BLOCK + jnp.where(first_half, lane[:1], lane[:1] - BLOCK)
    for i, b in enumerate((b0, b1)):
        both = jnp.where(first_half, start_row, swapped) if i == 0 else jnp.where(first_half, swapped, start_row)
        low = both - (b - BACK) * BLOCK
        bias[i] = jnp.where((key_place >= low) & (key_place <= high), 0.0, NEVER)

    for i in range(2):
        for head in range(GROUP):
            part = do_ref[i * BLOCK : (i + 1) * BLOCK, head * SPAN : (head + 1) * SPAN].astype(f32)
            dot_t[i, :, head * BLOCK : (head + 1) * BLOCK] = part.T

    await_bytes(r1.at[pl.ds(0, (ny - 1) * PLANE)], recv_sem.at[1])
    stored[...] = r1[...].astype(f32).reshape(blocks, 8, SPAN)
    seq[pl.ds(0, BACK)] = jnp.zeros((BACK, 8, SPAN), f32)

    def to_sequence(b, _):
        seq[b + BACK] = stored[place[0, b]]
        return 0

    lax.fori_loop(0, blocks, to_sequence, 0, unroll=8)
    first, second = pl.ds(0, PART + 8), pl.ds(PART + 8, PART - 8)

    def first_of(j):
        both = [seq[pl.ds(order[0, 2 * j], SEEN)], seq[pl.ds(order[0, 2 * j + 1], 1)]]
        return jnp.concatenate(both, axis=0).reshape(PART + 8, SPAN).astype(bf16)

    def second_of(j):
        return seq[pl.ds(order[0, 2 * j + 1] + 1, SEEN - 1)].reshape(PART - 8, SPAN).astype(bf16)

    def send_first(e):
        j = member(c, e)
        s2[e, first, :] = first_of(j)
        remote(s2.at[e, first, :], r2.at[rank_of(c), first, :], 3, {"ctx": j}).start()

    def send_second(e):
        j = member(c, e)
        s2[e, second, :] = second_of(j)
        remote(s2.at[e, second, :], r2.at[rank_of(c), second, :], 8, {"ctx": j}).start()

    for_each(1, CLASSES, send_first)
    for_each(1, CLASSES, send_second)
    r2[rank_of(c), first, :] = first_of(c)
    r2[rank_of(c), second, :] = second_of(c)
    peers = pl.ds(0, CLASSES - 1)
    some = pl.ds(0, (HEADS - 1) * rows)

    early, late = pl.ds(0, PART - 8), pl.ds(PART - 8, PART + 8)
    scale = SPAN ** (-0.5)
    power = scale * float(np.log2(np.e))
    for i in range(2):
        await_bytes(r2.at[peers, (first, second)[i], :], recv_sem.at[(3, 8)[i]])
        for kind, target in enumerate((keys, vals)):
            for piece in range(PIECES):
                near = r2[kind * PIECES + piece, i * (PART - 8) : i * (PART - 8) + PART + 8, :].astype(f32)
                target[i, piece * PART : (piece + 1) * PART, :] = near[8 * i : 8 * i + PART]
        if i == 0:
            await_bytes(q_loc.at[some, :], recv_sem.at[2])
        key_tile, value_tile = keys[i].astype(bf16), vals[i].astype(bf16)
        block = pl.ds(i * BLOCK, BLOCK)
        for part in range(GROUP * BLOCK // LANES):
            heads = range(part * LANES // BLOCK, (part + 1) * LANES // BLOCK)
            lanes = slice(part * LANES, (part + 1) * LANES)
            query = jnp.concatenate([q_loc[block, a * SPAN : (a + 1) * SPAN] for a in heads], axis=0)
            cotangent = jnp.concatenate([do_ref[block, a * SPAN : (a + 1) * SPAN] for a in heads], axis=0)
            scores = lax.dot_general(key_tile, query, NT, preferred_element_type=f32)
            scores = scores + jnp.concatenate([bias[i]] * (LANES // SPAN), axis=1)
            top = jnp.max(scores, axis=0, keepdims=True)
            raised = jnp.exp2((scores - top) * power)
            total = jnp.sum(raised, axis=0, keepdims=True)
            sums = lax.dot_general(value_tile, raised.astype(bf16), TN, preferred_element_type=f32)
            inverse = 1.0 / total
            attended = (sums * inverse).astype(bf16).astype(f32)
            dsum = jnp.sum(dot_t[i, :, lanes] * attended, axis=0, keepdims=True)
            prob = raised * inverse
            probs[:, lanes] = prob.astype(bf16)
            dprob = lax.dot_general(value_tile, cotangent, NT, preferred_element_type=f32)
            dscore = (prob * (dprob - dsum)).astype(bf16)
            dscores[:, lanes] = dscore
            query_grad = lax.dot_general(key_tile, dscore, TN, preferred_element_type=f32) * scale
            attended_rows = attended.T.astype(bf16)
            query_grad_rows = query_grad.T.astype(bf16)
            for n, a in enumerate(heads):
                att_out[block, a * SPAN : (a + 1) * SPAN] = attended_rows[n * BLOCK : (n + 1) * BLOCK]
                dq_loc[block, a * SPAN : (a + 1) * SPAN] = query_grad_rows[n * BLOCK : (n + 1) * BLOCK]
        query = jnp.concatenate([q_loc[block, a * SPAN : (a + 1) * SPAN] for a in range(GROUP)], axis=0)
        cotangent = jnp.concatenate([do_ref[block, a * SPAN : (a + 1) * SPAN] for a in range(GROUP)], axis=0)
        keys[i] = jnp.dot(dscores[...], query, preferred_element_type=f32) * scale
        vals[i] = jnp.dot(probs[...], cotangent, preferred_element_type=f32)


        part, which = ((early, 4), (late, 9))[i]
        for kind, source in enumerate((keys, vals)):
            for piece in range(PIECES):
                mine = source[i, piece * PART : (piece + 1) * PART, :]
                if i == 0:
                    s3[kind * PIECES + piece, early, :] = mine[: PART - 8].astype(bf16)
                else:
                    before = source[0, piece * PART + PART - 8 : (piece + 1) * PART, :]
                    s3[kind * PIECES + piece, late, :] = jnp.concatenate([before, mine], axis=0).astype(bf16)

        def send_back(e):
            j = member(c, e)
            remote(s3.at[rank_of(j), part, :], r3.at[rank_of(c), part, :], which, {"ctx": j}).start()

        for_each(1, CLASSES, send_back)
        r3[rank_of(c), part, :] = s3[rank_of(c), part, :]

    await_bytes(r3.at[peers, early, :], recv_sem.at[4])
    await_bytes(r3.at[peers, late, :], recv_sem.at[9])
    r3f[pl.ds(0, 2 * CLASSES)] = r3[...].astype(f32).reshape(2 * CLASSES, SEEN, 8, SPAN)
    r3f[2 * CLASSES] = jnp.zeros((SEEN, 8, SPAN), f32)

    def add_up(b, sums):
        s = place[0, b]
        j = s // 2
        slot = jnp.where(j // CLASSES == c // CLASSES, rank_of(j) * 2 + lax.rem(s, 2), 2 * CLASSES)
        new = r3f[slot]
        sums = [sums[k] + new[k] for k in range(SEEN)]
        acc[b] = sums[0]
        return tuple(sums[1:]) + (jnp.zeros((8, SPAN), f32),)

    sums = lax.fori_loop(0, blocks, add_up, tuple(jnp.zeros((8, SPAN), f32) for _ in range(SEEN)), unroll=4)
    for k in range(BACK):
        acc[blocks + k] = sums[k]

    def tiles_of(there):
        tiles = []
        for n in range(PLANE):
            both = [acc[order[0, 2 * (there * PLANE + n) + i] + BACK] for i in range(2)]
            tiles.append(jnp.concatenate(both, axis=0).astype(bf16))
        return jnp.stack(tiles)

    def send_sums(d):
        there = lax.rem(y + d, ny)
        s4[there] = tiles_of(there)
        remote(s4.at[there], r4.at[y], 6, {"ctx": there * PLANE + zx}).start()

    for_each(1, ny, send_sums)
    r4[y] = tiles_of(y)

    def send_dq(d):
        g = lax.rem(h + d, HEADS)
        remote(dq_loc.at[own_rows(g), :], dq_out.at[:, head_columns(h, wide)], 5, {"head": g}).start()

    for_each(1, HEADS, send_dq)
    dq_out[:, head_columns(h, wide)] = dq_loc[own_rows(h), :]

    await_bytes(r4.at[pl.ds(0, ny - 1)], recv_sem.at[6])
    parts = []
    for half in range(2):
        part = r4[half].astype(f32)
        for there in range(half + 2, ny, 2):
            part = part + r4[there].astype(f32)
        parts.append(part.reshape(2 * PLANE, 8, SPAN))
    summed[...] = jnp.concatenate(parts, axis=1).astype(bf16)

    for kind, out in enumerate((dk_out, dv_out)):

        def send_sum(d):
            n, half = lax.rem(zx + d // 2, PLANE), lax.rem(d, 2)
            remote(
                summed.at[2 * n + half], out.at[:, head_columns(h, SPAN)], 7,
                {"ctx": y * PLANE + n, "head": half * LINE + x},
            ).start()

        @pl.when(z == kind)
        def _():
            for_each(2, 2 * PLANE, send_sum)
            for half in range(2):

                @pl.when(half * LINE + x != h)
                def _():
                    send_sum(half)

                @pl.when(half * LINE + x == h)
                def _():
                    pltpu.make_async_copy(
                        summed.at[2 * zx + half], out.at[:, head_columns(h, SPAN)], recv_sem.at[7]
                    ).start()

    await_bytes(q_loc.at[some, :], recv_sem.at[5])
    await_bytes(dealt, recv_sem.at[7])
    await_bytes(r1.at[pl.ds(0, (ny - 1) * PLANE)], send_sem.at[1])
    await_bytes(q_loc.at[some, :], send_sem.at[2])
    await_bytes(r2.at[peers, first, :], send_sem.at[3])
    await_bytes(r2.at[peers, second, :], send_sem.at[8])
    await_bytes(r3.at[peers, early, :], send_sem.at[4])
    await_bytes(r3.at[peers, late, :], send_sem.at[9])
    await_bytes(q_loc.at[some, :], send_sem.at[5])
    await_bytes(r4.at[pl.ds(0, ny - 1)], send_sem.at[6])
    for which in (0, 7):

        @pl.when(own_deal)
        def _():
            await_bytes(dealt.at[pl.ds(0, 2 * PLANE - 1)], send_sem.at[which])

        @pl.when(jnp.logical_not(own_deal))
        def _():
            await_bytes(dealt, send_sem.at[which])


def shards(queries, keys, values, output_gradient, segment_ids, block_order):
    nc = lax.axis_size("ctx")
    wide, blocks = GROUP * SPAN, 2 * nc
    bf16, f32, i32 = jnp.bfloat16, jnp.float32, jnp.int32
    vmem = pl.BlockSpec(memory_space=pltpu.VMEM)
    anywhere = pl.BlockSpec(memory_space=pl.ANY)
    shapes = (
        jax.ShapeDtypeStruct((2 * BLOCK, wide), bf16),
        jax.ShapeDtypeStruct(queries.shape, bf16),
        jax.ShapeDtypeStruct(keys.shape, bf16),
        jax.ShapeDtypeStruct(values.shape, bf16),
    )
    return pl.pallas_call(
        functools.partial(kernel, nc),
        out_shape=shapes,
        in_specs=[anywhere] * 6,
        out_specs=(vmem, vmem, vmem, vmem),
        scratch_shapes=[
            pltpu.VMEM((2 * BLOCK, wide), bf16),
            pltpu.VMEM((2 * PLANE, 16, SPAN), bf16),
            pltpu.VMEM((2, PLANE, 16, SPAN), bf16),
            pltpu.VMEM((nc, 16, SPAN), bf16),
            pltpu.VMEM((blocks, 8, SPAN), f32),
            pltpu.VMEM((blocks + BACK, 8, SPAN), f32),
            pltpu.VMEM((CLASSES, 2 * PART, SPAN), bf16),
            pltpu.VMEM((CLASSES, 2 * PART, SPAN), bf16),
            pltpu.VMEM((2, WINDOW, SPAN), f32),
            pltpu.VMEM((2, WINDOW, SPAN), f32),
            pltpu.VMEM((2, SPAN, GROUP * BLOCK), f32),
            pltpu.VMEM((2, WINDOW, SPAN), f32),
            pltpu.VMEM((WINDOW, GROUP * BLOCK), bf16),
            pltpu.VMEM((WINDOW, GROUP * BLOCK), bf16),
            pltpu.VMEM((2 * BLOCK, wide), bf16),
            pltpu.VMEM((CLASSES, 2 * PART, SPAN), bf16),
            pltpu.VMEM((CLASSES, 2 * PART, SPAN), bf16),
            pltpu.VMEM((2 * CLASSES + 1, SEEN, 8, SPAN), f32),
            pltpu.VMEM((blocks + BACK, 8, SPAN), f32),
            pltpu.VMEM((nc // PLANE, PLANE, 16, SPAN), bf16),
            pltpu.VMEM((nc // PLANE, PLANE, 16, SPAN), bf16),
            pltpu.VMEM((2 * PLANE, 16, SPAN), bf16),
            pltpu.VMEM((2 * BLOCK, wide), bf16),
            pltpu.VMEM((nc, 2 * BLOCK), i32),
            pltpu.VMEM((1, blocks), i32),
            pltpu.VMEM((1, blocks), i32),
            pltpu.SMEM((1, blocks), i32),
            pltpu.SMEM((1, blocks), i32),
            pltpu.SemaphoreType.DMA((10,)),
            pltpu.SemaphoreType.DMA((10,)),
            pltpu.SemaphoreType.DMA((8,)),
        ],
        compiler_params=pltpu.CompilerParams(
            collective_id=0, has_side_effects=True, vmem_limit_bytes=63 * 1024 * 1024
        ),
    )(block_order.reshape(1, blocks), queries, keys, values, output_gradient, segment_ids.reshape(nc, 2 * BLOCK))


def solution(mesh):
    in_specs = (
        P(("ctx", "head"), None),
        P(("ctx", "head"), None),
        P(("ctx", "head"), None),
        P("ctx", "head"),
        P(),
        P(),
    )
    out_specs = (
        P("ctx", "head"),
        P(("ctx", "head"), None),
        P(("ctx", "head"), None),
        P(("ctx", "head"), None),
    )
    return jax.shard_map(shards, mesh=mesh, in_specs=in_specs, out_specs=out_specs, check_vma=False)
```

time: 77.8 us -> 70.3 us (0.904)
  Pallas kernels: 73 us -> 65.5 us
    pallas_call x1, Pallas kernels: 73 us -> 65.5 us  [shards(): pl.pallas_call(functools.partial(kernel, nc), out_shape=shapes, in_specs=...]
where the time goes in v3:
time: 70.3 us; the launch traced here: 70 us
  Pallas kernels  65.5 us (93%)
  local copies, waits for them, and re-layouts  3.86 us (5%)
    pallas_call x1, Pallas kernels, shards(): pl.pallas_call(functools.partial(kernel, nc), out_shape=shapes, in_specs=...  65.5 us
    unnamed x10, local copies, waits for them, and re-layouts  3.86 us

profile of v3, /device:TPU:1, one launch (start us, length us, event | category | flops | bytes accessed | tf_op | source)
XLA Modules:
  0.0 70.0 jit_solution(16546196616421420252)
XLA Ops:
  0.6 65.5 %shard_map.93 = (bf16[128,1024]{1,0:T(8,128)(2,1)}, bf16[16,8192]{1,0:T(8,128)(2,1)}, bf16[16,1024]{1,0:T(8,128)(2,1)}, bf16[16,1024]{1,0:T(8,128)(2,1)}) custom-call(s32[1,128]{1,0:T(1,128)} %bitcast.3, bf16[16,8192]{1,0:T(8,128)(2,1)} %q_ref.1, bf16[16,1024]{1,0:T(8,128)(2,1)} %k_ref.1, bf16[16,1024]{1,0:T(8,128)(2,1)} %v_ref.1, bf16[128,1024]{1,0:T(8,128)(2,1)} %do_hbm.1, ...), custom_call_target="tpu_custom_call" | custom-call | tf_op jit(solution)/shard_map/pallas_call | solution.py:416
  66.1 0.0 copy-start
  66.1 1.7 %copy.14 = bf16[128,1024]{1,0:T(8,128)(2,1)} copy(bf16[128,1024]{1,0:T(8,128)(2,1)} %get-tuple-element.8) | data formatting | bytes 524288
  67.8 0.0 copy-done
  67.8 0.0 copy-start.2
  67.8 0.7 %copy.15 = bf16[16,8192]{1,0:T(8,128)(2,1)} copy(bf16[16,8192]{1,0:T(8,128)(2,1)S(1)} %copy-done) | data formatting | bytes 524288
  68.5 0.1 copy-done.2
  68.6 0.0 copy-start.1
  68.6 0.6 copy.16
  69.2 0.2 copy-done.1
  69.4 0.6 copy.17
Async XLA Ops:
  66.1 1.7 %copy-start = (bf16[16,8192]{1,0:T(8,128)(2,1)S(1)}, bf16[16,8192]{1,0:T(8,128)(2,1)}, u32[]{:S(2)}) copy-start(bf16[16,8192]{1,0:T(8,128)(2,1)} %get-tuple-element.9) | copy-start | bytes 786436
  67.8 0.8 %copy-start.2 = (bf16[16,1024]{1,0:T(8,128)(2,1)S(1)}, bf16[16,1024]{1,0:T(8,128)(2,1)}, u32[]{:S(2)}) copy-start(bf16[16,1024]{1,0:T(8,128)(2,1)} %get-tuple-element.10) | copy-start | bytes 98308
  68.6 0.8 %copy-start.1 = (bf16[16,1024]{1,0:T(8,128)(2,1)S(1)}, bf16[16,1024]{1,0:T(8,128)(2,1)}, u32[]{:S(2)}) copy-start(bf16[16,1024]{1,0:T(8,128)(2,1)} %get-tuple-element.11) | copy-start | bytes 98308

commit v4 on v3

--- a/solution.py
+++ b/solution.py
@@ -69,6 +69,9 @@
             device_id=where, device_id_type=MESH,
         )
 
+    def far_first(k):
+        return 4 + (k // 2) * (1 - 2 * lax.rem(k, 2))
+
     def for_each(low, high, what):
         def step(d, _):
             what(d)
@@ -76,6 +79,9 @@
 
         lax.fori_loop(low, high, step, 0)
 
+    def far_plane(k):
+        return ny // 2 + (k // 2) * (1 - 2 * lax.rem(k, 2))
+
     barrier = pltpu.get_barrier_semaphore()
 
     def greet(where):
@@ -84,16 +90,16 @@
     def greet_dealer(d):
         greet({"ctx": y * PLANE + lax.rem(zx + d // 2, PLANE), "head": x + LINE * lax.rem(d, 2)})
 
-    for_each(2, 2 * PLANE, greet_dealer)
+    for_each(2, 2 * PLANE, lambda k: greet_dealer(2 * PLANE + 1 - k))
     for half in range(2):
 
         @pl.when(x + LINE * half != h)
         def _():
             greet({"ctx": c, "head": x + LINE * half})
 
-    for_each(1, CLASSES, lambda e: greet({"ctx": member(c, e)}))
-    for_each(1, ny, lambda d: greet({"ctx": lax.rem(c + d * PLANE, nc)}))
-    for_each(1, HEADS, lambda d: greet({"head": lax.rem(h + d, HEADS)}))
+    for_each(1, ny, lambda k: greet({"ctx": lax.rem(c + far_plane(k) * PLANE, nc)}))
+    for_each(1, HEADS, lambda k: greet({"head": lax.rem(h + far_first(k), HEADS)}))
+    for_each(1, CLASSES, lambda k: greet({"ctx": member(c, CLASSES - k)}))
 
     def own_rows(g):
         return pl.ds(pl.multiple_of(g * rows, rows), rows)
@@ -140,7 +146,7 @@
             g = lax.rem(h + d, HEADS)
             remote(source.at[:, head_columns(g, SPAN)], dealt.at[slot], 0, {"ctx": there, "head": g}).start()
 
-        for_each(1, HEADS, deal)
+        for_each(1, HEADS, lambda k: deal(far_first(k)))
         stays = own_deal & (z == kind)
 
         @pl.when(jnp.logical_not(stays))
@@ -164,14 +170,14 @@
         there = lax.rem(y + d, ny)
         remote(spread.at[lax.rem(there, 2)], r1.at[own_plane(y)], 1, {"ctx": there * PLANE + zx}).start()
 
-    for_each(1, ny, send_spread)
+    for_each(1, ny, lambda k: send_spread(far_plane(k)))
     r1[own_plane(y)] = spread[lax.rem(y, 2)]
 
     def send_q(d):
         g = lax.rem(h + d, HEADS)
         remote(q_ref.at[:, head_columns(g, wide)], q_loc.at[own_rows(h), :], 2, {"head": g}).start()
 
-    for_each(1, HEADS, send_q)
+    for_each(1, HEADS, lambda k: send_q(far_first(k)))
     for fetch in fetch_rest:
         fetch.wait()
     fetch_place.wait()
@@ -239,8 +245,8 @@
         s2[e, second, :] = second_of(j)
         remote(s2.at[e, second, :], r2.at[rank_of(c), second, :], 8, {"ctx": j}).start()
 
-    for_each(1, CLASSES, send_first)
-    for_each(1, CLASSES, send_second)
+    for_each(1, CLASSES, lambda k: send_first(CLASSES - k))
+    for_each(1, CLASSES, lambda k: send_second(CLASSES - k))
     r2[rank_of(c), first, :] = first_of(c)
     r2[rank_of(c), second, :] = second_of(c)
     peers = pl.ds(0, CLASSES - 1)
@@ -304,7 +310,7 @@
             j = member(c, e)
             remote(s3.at[rank_of(j), part, :], r3.at[rank_of(c), part, :], which, {"ctx": j}).start()
 
-        for_each(1, CLASSES, send_back)
+        for_each(1, CLASSES, lambda k: send_back(CLASSES - k))
         r3[rank_of(c), part, :] = s3[rank_of(c), part, :]
 
     await_bytes(r3.at[peers, early, :], recv_sem.at[4])
@@ -337,14 +343,14 @@
         s4[there] = tiles_of(there)
         remote(s4.at[there], r4.at[y], 6, {"ctx": there * PLANE + zx}).start()
 
-    for_each(1, ny, send_sums)
+    for_each(1, ny, lambda k: send_sums(far_plane(k)))
     r4[y] = tiles_of(y)
 
     def send_dq(d):
         g = lax.rem(h + d, HEADS)
         remote(dq_loc.at[own_rows(g), :], dq_out.at[:, head_columns(h, wide)], 5, {"head": g}).start()
 
-    for_each(1, HEADS, send_dq)
+    for_each(1, HEADS, lambda k: send_dq(far_first(k)))
     dq_out[:, head_columns(h, wide)] = dq_loc[own_rows(h), :]
 
     await_bytes(r4.at[pl.ds(0, ny - 1)], recv_sem.at[6])
@@ -452,9 +458,9 @@
             pltpu.SemaphoreType.DMA((8,)),
         ],
         compiler_params=pltpu.CompilerParams(
-            collective_id=0, has_side_effects=True, vmem_limit_bytes=63 * 1024 * 1024
+            collective_id=0, has_side_effects=True, vmem_limit_bytes=48 * 1024 * 1024
         ),
-    )(block_order.reshape(1, blocks), queries, keys, values, output_gradient, segment_ids.reshape(nc, 2 * BLOCK))
+    )(*(pltpu.with_memory_space_constraint(a, pltpu.HBM) for a in (block_order.reshape(1, blocks), queries, keys, values, output_gradient, segment_ids.reshape(nc, 2 * BLOCK))))
 
 
 def solution(mesh):

time: 70.3 us -> 67.1 us (0.954)
  Pallas kernels: 65.5 us -> 63.7 us
  local copies, waits for them, and re-layouts: 3.86 us -> 2.64 us
    pallas_call x1, Pallas kernels: 65.5 us -> 63.7 us  [shards(): pl.pallas_call(functools.partial(kernel, nc), out_shape=shapes, in_specs=...]
    unnamed x10 -> x4, local copies, waits for them, and re-layouts: 3.86 us -> 2.64 us
where the time goes in v4:
time: 67.1 us; the launch traced here: 66.9 us
  Pallas kernels  63.7 us (95%)
  local copies, waits for them, and re-layouts  2.64 us (4%)
    pallas_call x1, Pallas kernels, shards(): pl.pallas_call(functools.partial(kernel, nc), out_shape=shapes, in_specs=...  63.7 us
    unnamed x4, local copies, waits for them, and re-layouts  2.64 us

profile of v4, /device:TPU:1, one launch (start us, length us, event | category | flops | bytes accessed | tf_op | source)
XLA Modules:
  0.0 66.9 jit_solution(14641669747893988148)
XLA Ops:
  0.6 63.7 %shard_map.93 = (bf16[128,1024]{1,0:T(8,128)(2,1)S(1)}, bf16[16,8192]{1,0:T(8,128)(2,1)S(1)}, bf16[16,1024]{1,0:T(8,128)(2,1)S(1)}, bf16[16,1024]{1,0:T(8,128)(2,1)S(1)}) custom-call(s32[1,128]{1,0:T(1,128)} %bitcast.3, bf16[16,8192]{1,0:T(8,128)(2,1)} %q_ref.1, bf16[16,1024]{1,0:T(8,128)(2,1)} %k_ref.1, bf16[16,1024]{1,0:T(8,128)(2,1)} %v_ref.1, ...), custom_call_target="tpu_custom_call" | custom-call | tf_op jit(solution)/shard_map/pallas_call | solution.py:422
  64.3 0.7 %copy.14 = bf16[128,1024]{1,0:T(8,128)(2,1)} copy(bf16[128,1024]{1,0:T(8,128)(2,1)S(1)} %get-tuple-element.8) | data formatting | bytes 524288
  65.0 0.7 %copy.15 = bf16[16,8192]{1,0:T(8,128)(2,1)} copy(bf16[16,8192]{1,0:T(8,128)(2,1)S(1)} %get-tuple-element.9) | data formatting | bytes 524288
  65.7 0.6 copy.16
  66.3 0.6 copy.17

commit v5 on v4

--- a/solution.py
+++ b/solution.py
@@ -21,7 +21,6 @@
 CLASSES = 16
 PIECES = 8
 PART = SEEN * 8
-LANES = 256
 NEVER = -1e30
 
 MESH = pl.DeviceIdType.MESH
@@ -49,8 +48,8 @@
     order_hbm, q_ref, k_ref, v_ref, do_hbm, seg_hbm,
     att_out, dq_out, dk_out, dv_out,
     q_loc, dealt, spread, r1, stored, seq, s2, r2, keys, vals, dot_t, bias,
-    probs, dscores, dq_loc, s3, r3, r3f, acc, s4, r4, summed,
-    do_ref, seg_ref, order_row, place_row, order, place,
+    dscores, dq_loc, s3, r3, r3f, acc, s4, r4, summed,
+    do_ref, seg_ref, order_row, place_row, order, place, slots,
     send_sem, recv_sem, local_sem,
 ):
     c = lax.axis_index("ctx")
@@ -118,6 +117,35 @@
     ]
     for fetch in fetch_order + fetch_rest:
         fetch.start()
+    others = 2 * PLANE + CLASSES - 1 + ny - 1 + HEADS - 1
+
+    @pl.when(own_deal)
+    def _():
+        pl.semaphore_wait(barrier, others - 1)
+
+    @pl.when(jnp.logical_not(own_deal))
+    def _():
+        pl.semaphore_wait(barrier, others)
+
+    slot = zx * 2 + h // LINE
+    for kind, source in enumerate((k_ref, v_ref)):
+        there = (y * PAIR + kind) * LINE + lax.rem(h, LINE)
+
+        def deal(d):
+            g = lax.rem(h + d, HEADS)
+            remote(source.at[:, head_columns(g, SPAN)], dealt.at[slot], 0, {"ctx": there, "head": g}).start()
+
+        for_each(1, HEADS, lambda k: deal(far_first(k)))
+        stays = own_deal & (z == kind)
+
+        @pl.when(jnp.logical_not(stays))
+        def _():
+            deal(0)
+
+        @pl.when(stays)
+        def _():
+            pltpu.make_async_copy(source.at[:, head_columns(h, SPAN)], dealt.at[slot], recv_sem.at[0]).start()
+
     for fetch in fetch_order:
         fetch.wait()
 
@@ -127,35 +155,6 @@
     place_row[...] = jnp.max(jnp.where(order_col == across, spot, 0), axis=0, keepdims=True)
     fetch_place = pltpu.make_async_copy(place_row, place, local_sem.at[7])
     fetch_place.start()
-
-    others = 2 * PLANE + CLASSES - 1 + ny - 1 + HEADS - 1
-
-    @pl.when(own_deal)
-    def _():
-        pl.semaphore_wait(barrier, others - 1)
-
-    @pl.when(jnp.logical_not(own_deal))
-    def _():
-        pl.semaphore_wait(barrier, others)
-
-    slot = zx * 2 + h // LINE
-    for kind, source in enumerate((k_ref, v_ref)):
-        there = (y * PAIR + kind) * LINE + lax.rem(h, LINE)
-
-        def deal(d):
-            g = lax.rem(h + d, HEADS)
-            remote(source.at[:, head_columns(g, SPAN)], dealt.at[slot], 0, {"ctx": there, "head": g}).start()
-
-        for_each(1, HEADS, lambda k: deal(far_first(k)))
-        stays = own_deal & (z == kind)
-
-        @pl.when(jnp.logical_not(stays))
-        def _():
-            deal(0)
-
-        @pl.when(stays)
-        def _():
-            pltpu.make_async_copy(source.at[:, head_columns(h, SPAN)], dealt.at[slot], recv_sem.at[0]).start()
 
     await_bytes(dealt, recv_sem.at[0])
 
@@ -212,6 +211,14 @@
         low = both - (b - BACK) * BLOCK
         bias[i] = jnp.where((key_place >= low) & (key_place <= high), 0.0, NEVER)
 
+    def find_slot(b, _):
+        s = place[0, b]
+        j = s // 2
+        slots[0, b] = jnp.where(j // CLASSES == c // CLASSES, rank_of(j) * 2 + lax.rem(s, 2), 2 * CLASSES)
+        return 0
+
+    lax.fori_loop(0, blocks, find_slot, 0)
+
     for i in range(2):
         for head in range(GROUP):
             part = do_ref[i * BLOCK : (i + 1) * BLOCK, head * SPAN : (head + 1) * SPAN].astype(f32)
@@ -265,36 +272,24 @@
             await_bytes(q_loc.at[some, :], recv_sem.at[2])
         key_tile, value_tile = keys[i].astype(bf16), vals[i].astype(bf16)
         block = pl.ds(i * BLOCK, BLOCK)
-        for part in range(GROUP * BLOCK // LANES):
-            heads = range(part * LANES // BLOCK, (part + 1) * LANES // BLOCK)
-            lanes = slice(part * LANES, (part + 1) * LANES)
-            query = jnp.concatenate([q_loc[block, a * SPAN : (a + 1) * SPAN] for a in heads], axis=0)
-            cotangent = jnp.concatenate([do_ref[block, a * SPAN : (a + 1) * SPAN] for a in heads], axis=0)
-            scores = lax.dot_general(key_tile, query, NT, preferred_element_type=f32)
-            scores = scores + jnp.concatenate([bias[i]] * (LANES // SPAN), axis=1)
-            top = jnp.max(scores, axis=0, keepdims=True)
-            raised = jnp.exp2((scores - top) * power)
-            total = jnp.sum(raised, axis=0, keepdims=True)
-            sums = lax.dot_general(value_tile, raised.astype(bf16), TN, preferred_element_type=f32)
-            inverse = 1.0 / total
-            attended = (sums * inverse).astype(bf16).astype(f32)
-            dsum = jnp.sum(dot_t[i, :, lanes] * attended, axis=0, keepdims=True)
-            prob = raised * inverse
-            probs[:, lanes] = prob.astype(bf16)
-            dprob = lax.dot_general(value_tile, cotangent, NT, preferred_element_type=f32)
-            dscore = (prob * (dprob - dsum)).astype(bf16)
-            dscores[:, lanes] = dscore
-            query_grad = lax.dot_general(key_tile, dscore, TN, preferred_element_type=f32) * scale
-            attended_rows = attended.T.astype(bf16)
-            query_grad_rows = query_grad.T.astype(bf16)
-            for n, a in enumerate(heads):
-                att_out[block, a * SPAN : (a + 1) * SPAN] = attended_rows[n * BLOCK : (n + 1) * BLOCK]
-                dq_loc[block, a * SPAN : (a + 1) * SPAN] = query_grad_rows[n * BLOCK : (n + 1) * BLOCK]
-        query = jnp.concatenate([q_loc[block, a * SPAN : (a + 1) * SPAN] for a in range(GROUP)], axis=0)
-        cotangent = jnp.concatenate([do_ref[block, a * SPAN : (a + 1) * SPAN] for a in range(GROUP)], axis=0)
-        keys[i] = jnp.dot(dscores[...], query, preferred_element_type=f32) * scale
-        vals[i] = jnp.dot(probs[...], cotangent, preferred_element_type=f32)
-
+        heads = range(GROUP)
+        query = jnp.concatenate([q_loc[block, a * SPAN : (a + 1) * SPAN] for a in heads], axis=0)
+        cotangent = jnp.concatenate([do_ref[block, a * SPAN : (a + 1) * SPAN] for a in heads], axis=0)
+        scores = lax.dot_general(key_tile, query, NT, preferred_element_type=f32)
+        scores = scores + jnp.concatenate([bias[i]] * (GROUP * BLOCK // SPAN), axis=1)
+        top = jnp.max(scores, axis=0, keepdims=True)
+        raised = jnp.exp2((scores - top) * power)
+        total = jnp.sum(raised, axis=0, keepdims=True)
+        sums = lax.dot_general(value_tile, raised.astype(bf16), TN, preferred_element_type=f32)
+        inverse = 1.0 / total
+        attended = (sums * inverse).astype(bf16).astype(f32)
+        dsum = jnp.sum(dot_t[i] * attended, axis=0, keepdims=True)
+        prob = raised * inverse
+        vals[i] = jnp.dot(prob.astype(bf16), cotangent, preferred_element_type=f32)
+        dprob = lax.dot_general(value_tile, cotangent, NT, preferred_element_type=f32)
+        dscore = (prob * (dprob - dsum)).astype(bf16)
+        dscores[...] = dscore
+        keys[i] = jnp.dot(dscore, query, preferred_element_type=f32) * scale
 
         part, which = ((early, 4), (late, 9))[i]
         for kind, source in enumerate((keys, vals)):
@@ -313,16 +308,20 @@
         for_each(1, CLASSES, lambda k: send_back(CLASSES - k))
         r3[rank_of(c), part, :] = s3[rank_of(c), part, :]
 
+        query_grad = lax.dot_general(key_tile, dscores[...], TN, preferred_element_type=f32) * scale
+        attended_rows = attended.T.astype(bf16)
+        query_grad_rows = query_grad.T.astype(bf16)
+        for a in heads:
+            att_out[block, a * SPAN : (a + 1) * SPAN] = attended_rows[a * BLOCK : (a + 1) * BLOCK]
+            dq_loc[block, a * SPAN : (a + 1) * SPAN] = query_grad_rows[a * BLOCK : (a + 1) * BLOCK]
+
     await_bytes(r3.at[peers, early, :], recv_sem.at[4])
     await_bytes(r3.at[peers, late, :], recv_sem.at[9])
     r3f[pl.ds(0, 2 * CLASSES)] = r3[...].astype(f32).reshape(2 * CLASSES, SEEN, 8, SPAN)
     r3f[2 * CLASSES] = jnp.zeros((SEEN, 8, SPAN), f32)
 
     def add_up(b, sums):
-        s = place[0, b]
-        j = s // 2
-        slot = jnp.where(j // CLASSES == c // CLASSES, rank_of(j) * 2 + lax.rem(s, 2), 2 * CLASSES)
-        new = r3f[slot]
+        new = r3f[slots[0, b]]
         sums = [sums[k] + new[k] for k in range(SEEN)]
         acc[b] = sums[0]
         return tuple(sums[1:]) + (jnp.zeros((8, SPAN), f32),)
@@ -405,6 +404,15 @@
         @pl.when(jnp.logical_not(own_deal))
         def _():
             await_bytes(dealt, send_sem.at[which])
+
+
+def put(*refs):
+    sems = refs[-1]
+    copies = [pltpu.make_async_copy(a, b, sems.at[i]) for i, (a, b) in enumerate(zip(refs[:4], refs[4:8]))]
+    for copy in copies:
+        copy.start()
+    for copy in copies:
+        copy.wait()
 
 
 def shards(queries, keys, values, output_gradient, segment_ids, block_order):
@@ -419,7 +427,7 @@
         jax.ShapeDtypeStruct(keys.shape, bf16),
         jax.ShapeDtypeStruct(values.shape, bf16),
     )
-    return pl.pallas_call(
+    results = pl.pallas_call(
         functools.partial(kernel, nc),
         out_shape=shapes,
         in_specs=[anywhere] * 6,
@@ -438,7 +446,6 @@
             pltpu.VMEM((2, SPAN, GROUP * BLOCK), f32),
             pltpu.VMEM((2, WINDOW, SPAN), f32),
             pltpu.VMEM((WINDOW, GROUP * BLOCK), bf16),
-            pltpu.VMEM((WINDOW, GROUP * BLOCK), bf16),
             pltpu.VMEM((2 * BLOCK, wide), bf16),
             pltpu.VMEM((CLASSES, 2 * PART, SPAN), bf16),
             pltpu.VMEM((CLASSES, 2 * PART, SPAN), bf16),
@@ -453,6 +460,7 @@
             pltpu.VMEM((1, blocks), i32),
             pltpu.SMEM((1, blocks), i32),
             pltpu.SMEM((1, blocks), i32),
+            pltpu.SMEM((1, blocks), i32),
             pltpu.SemaphoreType.DMA((10,)),
             pltpu.SemaphoreType.DMA((10,)),
             pltpu.SemaphoreType.DMA((8,)),
@@ -461,6 +469,13 @@
             collective_id=0, has_side_effects=True, vmem_limit_bytes=48 * 1024 * 1024
         ),
     )(*(pltpu.with_memory_space_constraint(a, pltpu.HBM) for a in (block_order.reshape(1, blocks), queries, keys, values, output_gradient, segment_ids.reshape(nc, 2 * BLOCK))))
+    return pl.pallas_call(
+        put,
+        out_shape=shapes,
+        in_specs=[vmem] * 4,
+        out_specs=(pl.BlockSpec(memory_space=pltpu.HBM),) * 4,
+        scratch_shapes=[pltpu.SemaphoreType.DMA((4,))],
+    )(*(pltpu.with_memory_space_constraint(a, pltpu.VMEM) for a in results))
 
 
 def solution(mesh):

time: 67.1 us -> 62 us (0.924)
  local copies, waits for them, and re-layouts: 2.64 us -> 0 us
  Pallas kernels: 63.7 us -> 61.2 us
    pallas_call x1, Pallas kernels: 63.7 us -> 60.4 us  [shards(): pl.pallas_call(functools.partial(kernel, nc), out_shape=shapes, in_specs=...]
    unnamed x4 -> x0, local copies, waits for them, and re-layouts: 2.64 us -> none
    pallas_call x0 -> x1, Pallas kernels: none -> 0.84 us  [shards(): pl.pallas_call(put, out_shape=shapes, in_specs=[vmem] * 4, out_specs=(pl....]
where the time goes in v5:
time: 62 us; the launch traced here: 61.9 us
  Pallas kernels  61.2 us (99%)
  between operations  0.64 us (1%)
    pallas_call x1, Pallas kernels, shards(): pl.pallas_call(functools.partial(kernel, nc), out_shape=shapes, in_specs=...  60.4 us

profile of v5, /device:TPU:1, one launch (start us, length us, event | category | flops | bytes accessed | tf_op | source)
XLA Modules:
  0.0 61.9 jit_solution(8353866417390222574)
XLA Ops:
  0.6 60.4 %shard_map.93 = (bf16[128,1024]{1,0:T(8,128)(2,1)S(1)}, bf16[16,8192]{1,0:T(8,128)(2,1)S(1)}, bf16[16,1024]{1,0:T(8,128)(2,1)S(1)}, bf16[16,1024]{1,0:T(8,128)(2,1)S(1)}) custom-call(s32[1,128]{1,0:T(1,128)} %bitcast.3, bf16[16,8192]{1,0:T(8,128)(2,1)} %q_ref.1, bf16[16,1024]{1,0:T(8,128)(2,1)} %k_ref.1, bf16[16,1024]{1,0:T(8,128)(2,1)} %v_ref.1, ...), custom_call_target="tpu_custom_call" | custom-call | tf_op jit(solution)/shard_map/pallas_call | solution.py:430
  61.1 0.8 %shard_map.94 = (bf16[128,1024]{1,0:T(8,128)(2,1)}, bf16[16,8192]{1,0:T(8,128)(2,1)}, bf16[16,1024]{1,0:T(8,128)(2,1)}, bf16[16,1024]{1,0:T(8,128)(2,1)}) custom-call(bf16[128,1024]{1,0:T(8,128)(2,1)S(1)} %get-tuple-element.8.refs_0_, bf16[16,8192]{1,0:T(8,128)(2,1)S(1)} %get-tuple-element.9.refs_1_, bf16[16,1024]{1,0:T(8,128)(2,1)S(1)} %get-tuple-element.10.refs_2_, ...), custom_call_target="tpu_custom_call" | custom-call | tf_op jit(solution)/shard_map/pallas_call | solution.py:472

commit v6 on v5

--- a/solution.py
+++ b/solution.py
@@ -49,7 +49,7 @@
     att_out, dq_out, dk_out, dv_out,
     q_loc, dealt, spread, r1, stored, seq, s2, r2, keys, vals, dot_t, bias,
     dscores, dq_loc, s3, r3, r3f, acc, s4, r4, summed,
-    do_ref, seg_ref, order_row, place_row, order, place, slots,
+    k_near, v_near, do_ref, seg_ref, order_row, place_row, order, place, slots,
     send_sem, recv_sem, local_sem,
 ):
     c = lax.axis_index("ctx")
@@ -89,6 +89,12 @@
     def greet_dealer(d):
         greet({"ctx": y * PLANE + lax.rem(zx + d // 2, PLANE), "head": x + LINE * lax.rem(d, 2)})
 
+    fetch_kv = [
+        pltpu.make_async_copy(source, near, local_sem.at[kind])
+        for kind, (source, near) in enumerate(((k_ref, k_near), (v_ref, v_near)))
+    ]
+    for fetch in fetch_kv:
+        fetch.start()
     for_each(2, 2 * PLANE, lambda k: greet_dealer(2 * PLANE + 1 - k))
     for half in range(2):
 
@@ -117,6 +123,8 @@
     ]
     for fetch in fetch_order + fetch_rest:
         fetch.start()
+    for fetch in fetch_kv:
+        fetch.wait()
     others = 2 * PLANE + CLASSES - 1 + ny - 1 + HEADS - 1
 
     @pl.when(own_deal)
@@ -128,23 +136,28 @@
         pl.semaphore_wait(barrier, others)
 
     slot = zx * 2 + h // LINE
-    for kind, source in enumerate((k_ref, v_ref)):
+    near = (k_near, v_near)
+
+    def deal(kind, d):
+        g = lax.rem(h + d, HEADS)
         there = (y * PAIR + kind) * LINE + lax.rem(h, LINE)
-
-        def deal(d):
-            g = lax.rem(h + d, HEADS)
-            remote(source.at[:, head_columns(g, SPAN)], dealt.at[slot], 0, {"ctx": there, "head": g}).start()
-
-        for_each(1, HEADS, lambda k: deal(far_first(k)))
+        remote(near[kind].at[:, head_columns(g, SPAN)], dealt.at[slot], 0, {"ctx": there, "head": g}).start()
+
+    def deal_both(k):
+        deal(0, far_first(k))
+        deal(1, far_first(k))
+
+    for_each(1, HEADS, deal_both)
+    for kind in range(2):
         stays = own_deal & (z == kind)
 
         @pl.when(jnp.logical_not(stays))
         def _():
-            deal(0)
+            deal(kind, 0)
 
         @pl.when(stays)
         def _():
-            pltpu.make_async_copy(source.at[:, head_columns(h, SPAN)], dealt.at[slot], recv_sem.at[0]).start()
+            pltpu.make_async_copy(near[kind].at[:, head_columns(h, SPAN)], dealt.at[slot], recv_sem.at[0]).start()
 
     for fetch in fetch_order:
         fetch.wait()
@@ -372,7 +385,8 @@
 
         @pl.when(z == kind)
         def _():
-            for_each(2, 2 * PLANE, send_sum)
+            for_each(0, 12, lambda k: send_sum(2 * (2 + k // 4 - 3 * (k // 8)) + 8 * lax.rem(k // 2, 2) + lax.rem(k, 2)))
+            for_each(8, 10, send_sum)
             for half in range(2):
 
                 @pl.when(half * LINE + x != h)
@@ -454,6 +468,8 @@
             pltpu.VMEM((nc // PLANE, PLANE, 16, SPAN), bf16),
             pltpu.VMEM((nc // PLANE, PLANE, 16, SPAN), bf16),
             pltpu.VMEM((2 * PLANE, 16, SPAN), bf16),
+            pltpu.VMEM(keys.shape, bf16),
+            pltpu.VMEM(values.shape, bf16),
             pltpu.VMEM((2 * BLOCK, wide), bf16),
             pltpu.VMEM((nc, 2 * BLOCK), i32),
             pltpu.VMEM((1, blocks), i32),

time: 62 us -> 62 us (level)
  no operation moved by 1% of the time
where the time goes in v6:
time: 62 us; the launch traced here: 61.9 us
  Pallas kernels  61.3 us (99%)
  between operations  0.64 us (1%)
    pallas_call x1, Pallas kernels, shards(): pl.pallas_call(functools.partial(kernel, nc), out_shape=shapes, in_specs=...  60.4 us

profile of v6, /device:TPU:1, one launch (start us, length us, event | category | flops | bytes accessed | tf_op | source)
XLA Modules:
  0.0 61.9 jit_solution(8004009439771033332)
XLA Ops:
  0.6 60.4 %shard_map.93 = (bf16[128,1024]{1,0:T(8,128)(2,1)S(1)}, bf16[16,8192]{1,0:T(8,128)(2,1)S(1)}, bf16[16,1024]{1,0:T(8,128)(2,1)S(1)}, bf16[16,1024]{1,0:T(8,128)(2,1)S(1)}) custom-call(s32[1,128]{1,0:T(1,128)} %bitcast.3, bf16[16,8192]{1,0:T(8,128)(2,1)} %q_ref.1, bf16[16,1024]{1,0:T(8,128)(2,1)} %k_ref.1, bf16[16,1024]{1,0:T(8,128)(2,1)} %v_ref.1, ...), custom_call_target="tpu_custom_call" | custom-call | tf_op jit(solution)/shard_map/pallas_call | solution.py:444
  61.1 0.8 %shard_map.94 = (bf16[128,1024]{1,0:T(8,128)(2,1)}, bf16[16,8192]{1,0:T(8,128)(2,1)}, bf16[16,1024]{1,0:T(8,128)(2,1)}, bf16[16,1024]{1,0:T(8,128)(2,1)}) custom-call(bf16[128,1024]{1,0:T(8,128)(2,1)S(1)} %get-tuple-element.8.refs_0_, bf16[16,8192]{1,0:T(8,128)(2,1)S(1)} %get-tuple-element.9.refs_1_, bf16[16,1024]{1,0:T(8,128)(2,1)S(1)} %get-tuple-element.10.refs_2_, ...), custom_call_target="tpu_custom_call" | custom-call | tf_op jit(solution)/shard_map/pallas_call | solution.py:488

commit v7 on v6

--- a/solution.py
+++ b/solution.py
@@ -76,7 +76,7 @@
             what(d)
             return 0
 
-        lax.fori_loop(low, high, step, 0)
+        lax.fori_loop(low, high, step, 0, unroll=True)
 
     def far_plane(k):
         return ny // 2 + (k // 2) * (1 - 2 * lax.rem(k, 2))

time: 62 us -> 61.2 us (0.987)
  Pallas kernels: 61.3 us -> 60.4 us
    pallas_call x1, Pallas kernels: 60.4 us -> 59.6 us  [shards(): pl.pallas_call(functools.partial(kernel, nc), out_shape=shapes, in_specs=...]
where the time goes in v7:
time: 61.2 us; the launch traced here: 61 us
  Pallas kernels  60.4 us (99%)
  between operations  0.64 us (1%)
    pallas_call x1, Pallas kernels, shards(): pl.pallas_call(functools.partial(kernel, nc), out_shape=shapes, in_specs=...  59.6 us

profile of v7, /device:TPU:1, one launch (start us, length us, event | category | flops | bytes accessed | tf_op | source)
XLA Modules:
  0.0 61.0 jit_solution(15997012089811579208)
XLA Ops:
  0.6 59.6 %shard_map.93 = (bf16[128,1024]{1,0:T(8,128)(2,1)S(1)}, bf16[16,8192]{1,0:T(8,128)(2,1)S(1)}, bf16[16,1024]{1,0:T(8,128)(2,1)S(1)}, bf16[16,1024]{1,0:T(8,128)(2,1)S(1)}) custom-call(s32[1,128]{1,0:T(1,128)} %bitcast.3, bf16[16,8192]{1,0:T(8,128)(2,1)} %q_ref.1, bf16[16,1024]{1,0:T(8,128)(2,1)} %k_ref.1, bf16[16,1024]{1,0:T(8,128)(2,1)} %v_ref.1, ...), custom_call_target="tpu_custom_call" | custom-call | tf_op jit(solution)/shard_map/pallas_call | solution.py:444
  60.2 0.8 %shard_map.94 = (bf16[128,1024]{1,0:T(8,128)(2,1)}, bf16[16,8192]{1,0:T(8,128)(2,1)}, bf16[16,1024]{1,0:T(8,128)(2,1)}, bf16[16,1024]{1,0:T(8,128)(2,1)}) custom-call(bf16[128,1024]{1,0:T(8,128)(2,1)S(1)} %get-tuple-element.8.refs_0_, bf16[16,8192]{1,0:T(8,128)(2,1)S(1)} %get-tuple-element.9.refs_1_, bf16[16,1024]{1,0:T(8,128)(2,1)S(1)} %get-tuple-element.10.refs_2_, ...), custom_call_target="tpu_custom_call" | custom-call | tf_op jit(solution)/shard_map/pallas_call | solution.py:488

commit v8 on v7

--- a/solution.py
+++ b/solution.py
@@ -277,13 +277,16 @@
     power = scale * float(np.log2(np.e))
     for i in range(2):
         await_bytes(r2.at[peers, (first, second)[i], :], recv_sem.at[(3, 8)[i]])
-        for kind, target in enumerate((keys, vals)):
-            for piece in range(PIECES):
-                near = r2[kind * PIECES + piece, i * (PART - 8) : i * (PART - 8) + PART + 8, :].astype(f32)
-                target[i, piece * PART : (piece + 1) * PART, :] = near[8 * i : 8 * i + PART]
+        tiles = []
+        for kind in range(2):
+            pieces = [
+                r2[kind * PIECES + piece, i * (PART - 8) : i * (PART - 8) + PART + 8, :].astype(f32)[8 * i : 8 * i + PART]
+                for piece in range(PIECES)
+            ]
+            tiles.append(jnp.concatenate(pieces, axis=0).astype(bf16))
         if i == 0:
             await_bytes(q_loc.at[some, :], recv_sem.at[2])
-        key_tile, value_tile = keys[i].astype(bf16), vals[i].astype(bf16)
+        key_tile, value_tile = tiles
         block = pl.ds(i * BLOCK, BLOCK)
         heads = range(GROUP)
         query = jnp.concatenate([q_loc[block, a * SPAN : (a + 1) * SPAN] for a in heads], axis=0)

time: 61.2 us -> 61.3 us (level)
  no operation moved by 1% of the time
where the time goes in v8:
time: 61.3 us; the launch traced here: 61.1 us
  Pallas kernels  60.4 us (99%)
  between operations  0.64 us (1%)
    pallas_call x1, Pallas kernels, shards(): pl.pallas_call(functools.partial(kernel, nc), out_shape=shapes, in_specs=...  59.6 us

profile of v8, /device:TPU:1, one launch (start us, length us, event | category | flops | bytes accessed | tf_op | source)
XLA Modules:
  0.0 61.1 jit_solution(3423566129452750489)
XLA Ops:
  0.6 59.6 %shard_map.93 = (bf16[128,1024]{1,0:T(8,128)(2,1)S(1)}, bf16[16,8192]{1,0:T(8,128)(2,1)S(1)}, bf16[16,1024]{1,0:T(8,128)(2,1)S(1)}, bf16[16,1024]{1,0:T(8,128)(2,1)S(1)}) custom-call(s32[1,128]{1,0:T(1,128)} %bitcast.3, bf16[16,8192]{1,0:T(8,128)(2,1)} %q_ref.1, bf16[16,1024]{1,0:T(8,128)(2,1)} %k_ref.1, bf16[16,1024]{1,0:T(8,128)(2,1)} %v_ref.1, ...), custom_call_target="tpu_custom_call" | custom-call | tf_op jit(solution)/shard_map/pallas_call | solution.py:447
  60.2 0.8 %shard_map.94 = (bf16[128,1024]{1,0:T(8,128)(2,1)}, bf16[16,8192]{1,0:T(8,128)(2,1)}, bf16[16,1024]{1,0:T(8,128)(2,1)}, bf16[16,1024]{1,0:T(8,128)(2,1)}) custom-call(bf16[128,1024]{1,0:T(8,128)(2,1)S(1)} %get-tuple-element.8.refs_0_, bf16[16,8192]{1,0:T(8,128)(2,1)S(1)} %get-tuple-element.9.refs_1_, bf16[16,1024]{1,0:T(8,128)(2,1)S(1)} %get-tuple-element.10.refs_2_, ...), custom_call_target="tpu_custom_call" | custom-call | tf_op jit(solution)/shard_map/pallas_call | solution.py:491
